TPU v7x, 128 devices: a whole 4x4x4 slice. The times are simulated.
128 devices in a mesh: group: 4 (over z), front: 32 (over y, x, core).
Axes of the slice: x: 4, y: 4, z: 4, core: 2. Of those that a mesh axis runs over, the one named last changes fastest.
Arguments:
- front_matrix: float32 [4, 8192, 8192], P('group', 'front'), as said below
- child_tiles: bfloat16 [4, 4096, 128, 128], P('group', 'front'), may hold values from -4 to 4
- tile_route: int32 [4, 4096, 1], P('group', 'front'), may hold values from 0 to 103; in each aligned block of 128 rows (0 to 127, 128 to 255, ..., all dimensions but the last counted through in order) at most 2 rows name the same one
- tile_row: int32 [4, 4096], P('group', 'front'), may hold values from 0 to 1
- tile_col: int32 [4, 4096], P('group', 'front'), may hold values from 0 to 63
Outputs:
- factor: float32 [4, 8192, 1536], P('group', 'front')
- schur: float32 [4, 8192, 6656], P('group', 'front')
Inputs may be any that keep to these rules, and one draw needn't show every extreme that they name: Each front_matrix block is symmetric and positive definite. `tile_route`: among the 128 tiles of one device no value appears more than 2 times.
All inputs are finite; a program needn't handle non-finite values.
Results may differ from a plain program's by a relative error of at most 0.022.
Values may be sent and summed in bfloat16 or wider, within the bound.
A program may use at most 192 MiB of HBM per device.

v0:
```python
import jax
import jax.numpy as jnp
from jax import lax
from jax.sharding import PartitionSpec as P

PANELS = 6


def spread(x, axis, root):
    mine = lax.axis_index(axis) == root
    return lax.psum(jnp.where(mine, x, jnp.zeros_like(x)), axis)


def contract_rows(left_rows, right_rows):
    return lax.dot_general(
        left_rows, right_rows, (((1,), (1,)), ((), ())), preferred_element_type=jnp.float32
    )


def on_device(front_matrix, child_tiles, tile_route, tile_row, tile_col):
    work = front_matrix[0]
    width = work.shape[0]
    order = work.shape[1]
    tiles = child_tiles[0]
    count = tiles.shape[0]
    edge = tiles.shape[1]
    groups = lax.axis_size("group")
    fronts = lax.axis_size("front")
    devices = groups * fronts
    tail = fronts - PANELS
    target = tile_route[0, :, 0]
    destination = target // tail * fronts + PANELS + target % tail
    same_dest = destination[:, None] == destination[None, :]
    positions = jnp.arange(count)
    earlier = positions[None, :] < positions[:, None]
    slot_index = jnp.sum(jnp.where(same_dest & earlier, 1, 0), axis=1).astype(jnp.int32)
    depth = max(2, -(-count // (groups * tail)))
    outbox = (
        jnp.zeros((devices, depth, edge, edge), jnp.bfloat16).at[destination, slot_index].set(tiles)
    )
    labels = jnp.full((devices, depth, 2), width // edge, jnp.int32)
    labels = labels.at[destination, slot_index].set(jnp.stack([tile_row[0], tile_col[0]], axis=1))
    inbox, tags = (
        lax.all_to_all(outbox, ("group", "front"), split_axis=0, concat_axis=0, tiled=True),
        lax.all_to_all(labels, ("group", "front"), split_axis=0, concat_axis=0, tiled=True),
    )
    inbox = inbox.reshape(devices * depth, edge, edge)
    tags = tags.reshape(devices * depth, 2)
    blocks = work.reshape(width // edge, edge, order // edge, edge)
    blocks = blocks.at[tags[:, 0], :, tags[:, 1], :].add(inbox.astype(jnp.float32), mode="drop")
    work = blocks.reshape(width, order)
    position = lax.axis_index("front")
    pivots = PANELS * width
    factor = jnp.zeros((width, pivots), jnp.float32)
    for k in range(PANELS):
        first = k * width
        pivot = spread(work[:, first : first + width].astype(jnp.bfloat16), "front", k).astype(
            jnp.float32
        )
        lower_block = jnp.linalg.cholesky(pivot)
        solved = lax.linalg.triangular_solve(
            lower_block,
            work[:, first : first + width],
            left_side=False,
            lower=True,
            transpose_a=True,
        )
        column = jnp.where(position > k, solved, jnp.where(position == k, lower_block, 0.0))
        factor = factor.at[:, first : first + width].set(column)
        panel_bits = column.astype(jnp.bfloat16)

        def panel_terms(piece, start, panel_bits=panel_bits):
            return contract_rows(panel_bits, piece)

        work = work - panel_terms(
            lax.all_gather(panel_bits, "front", axis=0, tiled=True), jnp.int32(0)
        )
    remainder = work[:, pivots:]
    schur = jnp.where(position >= PANELS, remainder, 0.0)
    return (factor[None], schur[None])


def solution(mesh):
    return jax.shard_map(
        on_device,
        mesh=mesh,
        in_specs=(
            P("group", "front", None),
            P("group", "front", None, None),
            P("group", "front", None),
            P("group", "front"),
            P("group", "front"),
        ),
        out_specs=(P("group", "front", None), P("group", "front", None)),
        check_vma=False,
    )
```

profile of v0, /device:TPU:1, one launch (start us, length us, event | category | flops | bytes accessed | tf_op | source)
XLA Modules:
  0.0 1624.5 jit_solution(9090667161290281528)
XLA Ops:
  10.2 13.8 scatter_fusion
  24.0 11.5 all-to-all-start
  35.5 5.3 broadcast_in_dim.52
  40.8 20.7 %scatter_fusion.1 = bf16[128,2,128,128]{3,2,1,0:T(8,128)(2,1)} fusion(bf16[128,2,128,128]{3,2,1,0:T(8,128)(2,1)} %broadcast_in_dim.52, s32[128]{0:T(128)S(1)} %fusion.80, bf16[128,128,128]{2,1,0:T(8,128)(2,1)} %bitcast.271), kind=kCustom, calls=%fused_computation.1 | custom fusion | bytes 12583936 | tf_op jit(solution)/shard_map/scatter | solution.py:39
  61.5 10.2 all-to-all-start.1
  72.0 5.0 copy.158
  77.0 8.1 copy.92
  85.4 85.1 %all-to-all-done.1 = bf16[128,2,128,128]{3,2,1,0:T(8,128)(2,1)} async-done(((bf16[128,2,128,128]{3,2,1,0:T(8,128)(2,1)}), bf16[128,2,128,128]{3,2,1,0:T(8,128)(2,1)}, u32[]{:S(2)}, u32[]{:S(2)}) %all-to-all-start.1) | async-done | bytes 8388640 | tf_op jit(solution)/shard_map/all_to_all | solution.py:44
  170.4 11.2 bitcast_convert_fusion
  181.7 54.9 %scatter_fusion.2 = f32[2,128,64,128]{3,1,2,0:T(8,128)} fusion(f32[2,128,64,128]{3,1,2,0:T(8,128)} %copy.92, s32[256]{0:T(256)S(1)} %bitcast.265, f32[256,128,128]{2,1,0:T(8,128)} %bitcast_convert_fusion), kind=kCustom, calls=%fused_computation.2 | custom fusion | flops 4194304 | bytes 50333696 | tf_op jit(solution)/shard_map/scatter-add | solution.py:50
  236.5 13.2 copy.93
  249.7 3.9 copy.163
  257.8 102.0 %all-reduce.9.cloned.1.call-done = bf16[256,256]{0,1:T(8,128)(2,1)} async-done(((bf16[256,256]{0,1:T(8,128)(2,1)}), bf16[256,256]{0,1:T(8,128)(2,1)}) %all-reduce.9.cloned.1.call-update) | async-done | bytes 131088 | tf_op jit(solution)/shard_map/psum | solution.py:11
  361.8 11.7 cholesky.298
  373.6 9.8 custom-call.27
  384.0 11.7 cholesky.315
  397.9 4.1 while.18
  402.0 19.7 %custom-call.28 = f32[2,128,128]{1,2,0:T(8,128)S(1)} custom-call(f32[2,128,128]{2,1,0:T(8,128)S(1)} %get-tuple-element.114), custom_call_target="InvertDiagBlocksLowerTriangular" | custom-call | tf_op jit(solution)/shard_map/triangular_solve/custom-call.0 | solution.py:61
  425.2 49.4 %all-gather.7.cloned.1.call-done = bf16[8192,256]{0,1:T(8,128)(2,1)} async-done(((bf16[256,256]{0,1:T(8,128)(2,1)}), bf16[8192,256]{0,1:T(8,128)(2,1)}) %all-gather.7.cloned.1.call-update) | async-done | bytes 4194320 | tf_op jit(solution)/shard_map/all_gather | solution.py:76
  474.6 6.5 convolution_subtract_fusion.4
  481.1 3.2 copy-done.3
  485.6 98.3 %all-reduce.11.cloned.1.call-done = bf16[256,256]{0,1:T(8,128)(2,1)} async-done(((bf16[256,256]{0,1:T(8,128)(2,1)}), bf16[256,256]{0,1:T(8,128)(2,1)}) %all-reduce.11.cloned.1.call-update) | async-done | bytes 131088 | tf_op jit(solution)/shard_map/psum | solution.py:11
  585.8 11.7 cholesky.332
  597.7 9.8 custom-call.29
  608.1 11.7 cholesky.349
  622.5 4.3 while.19
  626.7 19.7 %custom-call.30 = f32[2,128,128]{1,2,0:T(8,128)S(1)} custom-call(f32[2,128,128]{2,1,0:T(8,128)S(1)} %get-tuple-element.115), custom_call_target="InvertDiagBlocksLowerTriangular" | custom-call | tf_op jit(solution)/shard_map/triangular_solve/custom-call.0 | solution.py:61
  650.0 49.4 %all-gather.9.cloned.1.call-done = bf16[8192,256]{0,1:T(8,128)(2,1)} async-done(((bf16[256,256]{0,1:T(8,128)(2,1)}), bf16[8192,256]{0,1:T(8,128)(2,1)}) %all-gather.9.cloned.1.call-update) | async-done | bytes 4194320 | tf_op jit(solution)/shard_map/all_gather | solution.py:76
  699.4 6.5 convolution_subtract_fusion.3
  709.8 98.8 %all-reduce.13.cloned.1.call-done = bf16[256,256]{0,1:T(8,128)(2,1)} async-done(((bf16[256,256]{0,1:T(8,128)(2,1)}), bf16[256,256]{0,1:T(8,128)(2,1)}) %all-reduce.13.cloned.1.call-update) | async-done | bytes 131088 | tf_op jit(solution)/shard_map/psum | solution.py:11
  810.6 11.7 cholesky.366
  822.4 9.8 custom-call.31
  832.8 11.7 cholesky.383
  847.2 4.5 while.20
  851.7 19.7 %custom-call.32 = f32[2,128,128]{1,2,0:T(8,128)S(1)} custom-call(f32[2,128,128]{2,1,0:T(8,128)S(1)} %get-tuple-element.116), custom_call_target="InvertDiagBlocksLowerTriangular" | custom-call | tf_op jit(solution)/shard_map/triangular_solve/custom-call.0 | solution.py:61
  875.0 49.4 %all-gather.11.cloned.1.call-done = bf16[8192,256]{0,1:T(8,128)(2,1)} async-done(((bf16[256,256]{0,1:T(8,128)(2,1)}), bf16[8192,256]{0,1:T(8,128)(2,1)}) %all-gather.11.cloned.1.call-update) | async-done | bytes 4194320 | tf_op jit(solution)/shard_map/all_gather | solution.py:76
  924.4 6.5 convolution_subtract_fusion.2
  934.8 98.7 %all-reduce.15.cloned.1.call-done = bf16[256,256]{0,1:T(8,128)(2,1)} async-done(((bf16[256,256]{0,1:T(8,128)(2,1)}), bf16[256,256]{0,1:T(8,128)(2,1)}) %all-reduce.15.cloned.1.call-update) | async-done | bytes 131088 | tf_op jit(solution)/shard_map/psum | solution.py:11
  1035.5 11.7 cholesky.400
  1047.4 9.8 custom-call.33
  1057.8 11.7 cholesky.417
  1072.2 4.3 while.21
  1076.5 19.7 %custom-call.34 = f32[2,128,128]{1,2,0:T(8,128)S(1)} custom-call(f32[2,128,128]{2,1,0:T(8,128)S(1)} %get-tuple-element.117), custom_call_target="InvertDiagBlocksLowerTriangular" | custom-call | tf_op jit(solution)/shard_map/triangular_solve/custom-call.0 | solution.py:61
  1099.7 49.4 %all-gather.13.cloned.1.call-done = bf16[8192,256]{0,1:T(8,128)(2,1)} async-done(((bf16[256,256]{0,1:T(8,128)(2,1)}), bf16[8192,256]{0,1:T(8,128)(2,1)}) %all-gather.13.cloned.1.call-update) | async-done | bytes 4194320 | tf_op jit(solution)/shard_map/all_gather | solution.py:76
  1149.1 6.5 convolution_subtract_fusion.1
  1155.6 3.2 copy-done.2
  1159.5 98.8 %all-reduce.17.cloned.1.call-done = bf16[256,256]{0,1:T(8,128)(2,1)} async-done(((bf16[256,256]{0,1:T(8,128)(2,1)}), bf16[256,256]{0,1:T(8,128)(2,1)}) %all-reduce.17.cloned.1.call-update) | async-done | bytes 131088 | tf_op jit(solution)/shard_map/psum | solution.py:11
  1260.3 11.7 cholesky.434
  1272.1 9.8 custom-call.35
  1282.5 11.7 cholesky.451
  1297.0 4.5 while.22
  1301.4 19.7 %custom-call.36 = f32[2,128,128]{1,2,0:T(8,128)S(1)} custom-call(f32[2,128,128]{2,1,0:T(8,128)S(1)} %get-tuple-element.118), custom_call_target="InvertDiagBlocksLowerTriangular" | custom-call | tf_op jit(solution)/shard_map/triangular_solve/custom-call.0 | solution.py:61
  1324.7 49.4 %all-gather.15.cloned.1.call-done = bf16[8192,256]{0,1:T(8,128)(2,1)} async-done(((bf16[256,256]{0,1:T(8,128)(2,1)}), bf16[8192,256]{0,1:T(8,128)(2,1)}) %all-gather.15.cloned.1.call-update) | async-done | bytes 4194320 | tf_op jit(solution)/shard_map/all_gather | solution.py:76
  1374.1 6.5 convolution_subtract_fusion
  1384.5 98.7 %all-reduce.19.cloned.1.call-done = bf16[256,256]{0,1:T(8,128)(2,1)} async-done(((bf16[256,256]{0,1:T(8,128)(2,1)}), bf16[256,256]{0,1:T(8,128)(2,1)}) %all-reduce.19.cloned.1.call-update) | async-done | bytes 131088 | tf_op jit(solution)/shard_map/psum | solution.py:11
  1485.2 11.7 cholesky.468
  1497.1 9.8 custom-call.37
  1507.5 11.7 cholesky.485
  1521.9 4.3 while.23
  1526.2 19.7 %custom-call.38 = f32[2,128,128]{1,2,0:T(8,128)S(1)} custom-call(f32[2,128,128]{2,1,0:T(8,128)S(1)} %get-tuple-element.119), custom_call_target="InvertDiagBlocksLowerTriangular" | custom-call | tf_op jit(solution)/shard_map/triangular_solve/custom-call.0 | solution.py:61
  1558.3 40.6 %all-gather.17.cloned.1.call-done = bf16[8192,256]{0,1:T(8,128)(2,1)} async-done(((bf16[256,256]{0,1:T(8,128)(2,1)}), bf16[8192,256]{0,1:T(8,128)(2,1)}) %all-gather.17.cloned.1.call-update) | async-done | bytes 4194320 | tf_op jit(solution)/shard_map/all_gather | solution.py:76
  1598.8 4.0 fusion.88
  1602.8 6.7 fusion.1
  1609.4 8.1 copy.137
  (254 shorter events, 99.2 us)
Async XLA Ops:
  24.0 37.6 %all-to-all-start = ((s32[128,2,2]{2,1,0:T(2,128)}), s32[128,2,2]{2,1,0:T(2,128)S(1)}, u32[]{:S(2)}, u32[]{:S(2)}) async-start(s32[128,2,2]{2,1,0:T(2,128)} %scatter_fusion), calls=%async_computation | async-start | bytes 262144 | tf_op jit(solution)/shard_map/all_to_all | solution.py:45
  61.5 108.9 %all-to-all-start.1 = ((bf16[128,2,128,128]{3,2,1,0:T(8,128)(2,1)}), bf16[128,2,128,128]{3,2,1,0:T(8,128)(2,1)}, u32[]{:S(2)}, u32[]{:S(2)}) async-start(bf16[128,2,128,128]{3,2,1,0:T(8,128)(2,1)} %scatter_fusion.1), calls=%async_computation.1 | async-start | bytes 16777216 | tf_op jit(solution)/shard_map/all_to_all | solution.py:44
  71.8 288.1 %all-reduce.9.cloned.1.call-start = ((), (), s32[]{:S(2)}) async-start(), calls=%async_computation.2 | async-start | bytes 262144 | tf_op jit(solution)/shard_map/psum | solution.py:11
  253.6 3.2 copy-start.5
  257.5 217.1 %all-gather.7.cloned.1.call-start = ((), (), s32[]{:S(2)}) async-start(), calls=%async_computation.3 | async-start | bytes 4325376 | tf_op jit(solution)/shard_map/all_gather | solution.py:76
  425.2 158.7 %all-reduce.11.cloned.1.call-start = ((), (), s32[]{:S(2)}) async-start(), calls=%async_computation.4 | async-start | bytes 262144 | tf_op jit(solution)/shard_map/psum | solution.py:11
  481.1 3.2 copy-start.3
  485.0 214.4 %all-gather.9.cloned.1.call-start = ((), (), s32[]{:S(2)}) async-start(), calls=%async_computation.5 | async-start | bytes 4325376 | tf_op jit(solution)/shard_map/all_gather | solution.py:76
  649.9 158.7 %all-reduce.13.cloned.1.call-start = ((), (), s32[]{:S(2)}) async-start(), calls=%async_computation.6 | async-start | bytes 262144 | tf_op jit(solution)/shard_map/psum | solution.py:11
  705.9 3.2 copy-start
  709.8 214.6 %all-gather.11.cloned.1.call-start = ((), (), s32[]{:S(2)}) async-start(), calls=%async_computation.7 | async-start | bytes 4325376 | tf_op jit(solution)/shard_map/all_gather | solution.py:76
  874.9 158.6 %all-reduce.15.cloned.1.call-start = ((), (), s32[]{:S(2)}) async-start(), calls=%async_computation.8 | async-start | bytes 262144 | tf_op jit(solution)/shard_map/psum | solution.py:11
  930.9 3.2 copy-start.1
  934.8 214.3 %all-gather.13.cloned.1.call-start = ((), (), s32[]{:S(2)}) async-start(), calls=%async_computation.9 | async-start | bytes 4325376 | tf_op jit(solution)/shard_map/all_gather | solution.py:76
  1099.6 158.7 %all-reduce.17.cloned.1.call-start = ((), (), s32[]{:S(2)}) async-start(), calls=%async_computation.10 | async-start | bytes 262144 | tf_op jit(solution)/shard_map/psum | solution.py:11
  1155.6 3.2 copy-start.2
  1159.5 214.6 %all-gather.15.cloned.1.call-start = ((), (), s32[]{:S(2)}) async-start(), calls=%async_computation.11 | async-start | bytes 4325376 | tf_op jit(solution)/shard_map/all_gather | solution.py:76
  1324.6 158.6 %all-reduce.19.cloned.1.call-start = ((), (), s32[]{:S(2)}) async-start(), calls=%async_computation.12 | async-start | bytes 262144 | tf_op jit(solution)/shard_map/psum | solution.py:11
  1380.6 3.2 copy-start.4
  1384.5 214.3 %all-gather.17.cloned.1.call-start = ((), (), s32[]{:S(2)}) async-start(), calls=%async_computation.13 | async-start | bytes 4325376 | tf_op jit(solution)/shard_map/all_gather | solution.py:76
  1549.3 49.5 %copy-start.6 = (bf16[256,256]{0,1:T(8,128)(2,1)S(1)}, bf16[256,256]{0,1:T(8,128)(2,1)}, u32[]{:S(2)}) copy-start(bf16[256,256]{0,1:T(8,128)(2,1)} %fusion.68) | copy-start | bytes 393220
Sparse Core Ops, SparseCore 0:
  257.7 102.1 all-reduce.8
  425.3 49.2 all-gather.6
  485.2 98.6 all-reduce.10
  650.0 49.2 all-gather.8
  709.9 98.6 all-reduce.12
  875.0 49.2 all-gather.10
  934.9 98.6 all-reduce.14
  1099.8 49.2 all-gather.12
  1159.6 98.6 all-reduce.16
  1324.7 49.2 all-gather.14
  1384.6 98.6 all-reduce.18
  1549.5 49.2 all-gather.16
where the time goes:
time: 1630 us; the launch traced here: 1620 us
  waiting for transfers between devices  968 us (59%)
  other arithmetic  421 us (26%)
  local copies, waits for them, and re-layouts  132 us (8%)
  matrix products  55.7 us (3%)
  starting transfers between devices  23.1 us (1%)
  between operations  22.8 us (1%)
    psum x6, waiting for transfers between devices, spread(): return lax.psum(jnp.where(mine, x, jnp.zeros_like(x)), axis)  595 us
    all_gather x6, waiting for transfers between devices, on_device(): lax.all_gather(panel_bits, 'front', axis=0, tiled=True)  288 us
    another operation x41, other arithmetic, on_device(): lower_block = jnp.linalg.cholesky(pivot)  207 us
    another operation x13, other arithmetic, on_device(): lax.linalg.triangular_solve(lower_block, work[:, first:first + width], le...  118 us
    all_to_all x1, waiting for transfers between devices, on_device(): lax.all_to_all(outbox, ('group', 'front'), split_axis=0, concat_axis=0, t...  85.1 us
    scatter-add x1, other arithmetic, on_device(): blocks.at[tags[:, 0], :, tags[:, 1], :]  54.9 us
    unnamed x21, local copies, waits for them, and re-layouts  38.2 us
    dot_general x6, matrix products, contract_rows(): lax.dot_general(left_rows, right_rows, (((1,), (1,)), ((), ())), preferre...  36.3 us
  transfers between devices with their start and end apart: 14, of which 13 were waited for; matrix products, arithmetic and copies ran while one was open for 3% of the time, Pallas kernels for 0%

commit v1 on v0

v1 whole, which is shorter than its diff:
```python
import functools

import jax
import jax.numpy as jnp
from jax import lax
from jax.experimental import pallas as pl
from jax.experimental.pallas import tpu as pltpu
from jax.sharding import PartitionSpec as P

PANELS = 6
PW = 256
TB = 128
SUB = 16
SLOTS = 2
MIB = 1 << 20


def dot_nt(a, b, precision=None):
    return lax.dot_general(
        a, b, (((1,), (1,)), ((), ())), precision=precision, preferred_element_type=jnp.float32
    )


def dot_nn(a, b, precision=None):
    return lax.dot_general(
        a, b, (((1,), (0,)), ((), ())), precision=precision, preferred_element_type=jnp.float32
    )


def halves(a):
    high = a.astype(jnp.bfloat16)
    low = (a - high.astype(jnp.float32)).astype(jnp.bfloat16)
    return high, low


def dot_tn_split(a, b):
    ah, al = halves(a)
    bh, bl = halves(b)
    left = jnp.concatenate([ah, ah, al], axis=0)
    right = jnp.concatenate([bh, bl, bh], axis=0)
    return lax.dot_general(
        left, right, (((0,), (0,)), ((), ())), preferred_element_type=jnp.float32
    )


def dot_nt_split(a, b):
    ah, al = halves(a)
    bh, bl = halves(b)
    left = jnp.concatenate([ah, ah, al], axis=1)
    right = jnp.concatenate([bh, bl, bh], axis=1)
    return dot_nt(left, right)


def dot_nn_split(a, b):
    ah, al = halves(a)
    bh, bl = halves(b)
    left = jnp.concatenate([ah, ah, al], axis=1)
    right = jnp.concatenate([bh, bl, bh], axis=0)
    return dot_nn(left, right)


def chol_inv(block):
    n = TB
    parts = SUB // 8
    lane = lax.broadcasted_iota(jnp.int32, (8, n), 1)
    sub = lax.broadcasted_iota(jnp.int32, (8, n), 0)
    rows = [block[8 * i : 8 * i + 8] for i in range(n // 8)]
    upper = []
    inverse = []
    for p in range(n // SUB):
        first = p * parts
        left = p * SUB
        panel = rows[first : first + parts]
        unit = [jnp.where(lane == sub + (left + 8 * h), 1.0, 0.0) for h in range(parts)]
        spread = [
            [jnp.broadcast_to(panel[h][:, left + j : left + j + 1], (8, n)) for h in range(parts)]
            for j in range(SUB)
        ]
        scale = [jnp.zeros((8, n), jnp.float32) for _ in range(parts)]
        for j in range(SUB):
            at, s = divmod(j, 8)
            inv = lax.rsqrt(jnp.broadcast_to(spread[j][at][s : s + 1], (8, n)))
            mult = [None] * parts
            for h in range(at, parts):
                mult[h] = spread[j][h] * inv
                if h == at:
                    mult[h] = jnp.where(sub > s, mult[h], 0.0)
            for target in [panel, unit] + spread[j + 1 :]:
                row = jnp.broadcast_to(target[at][s : s + 1], (8, n)) * inv
                for h in range(at, parts):
                    target[h] = target[h] - mult[h] * row
            scale[at] = jnp.where(sub == s, inv, scale[at])
        inside = (lane >= left) & (lane < left + SUB)
        ups = []
        full = []
        for h in range(parts):
            up = panel[h] * scale[h]
            mixed = jnp.where(inside, unit[h] * scale[h], up)
            inverse.append(jnp.where(lane < left + SUB, mixed, 0.0))
            upper.append(jnp.where(lane >= left, up, 0.0))
            ups.append(up)
            full.append(mixed)
        if left + SUB < n:
            ups = jnp.concatenate(ups, axis=0)
            full = jnp.concatenate(full, axis=0)
            change = dot_tn_split(ups[:, left + SUB :], full)
            for k, i in enumerate(range(first + parts, n // 8)):
                rows[i] = jnp.where(inside, 0.0, rows[i]) - change[8 * k : 8 * k + 8]
    return jnp.concatenate(upper, axis=0), jnp.concatenate(inverse, axis=0)


def pivot_kernel(me_ref, lead_ref, bits_ref, inverse_ref, own_ref, work, sem):
    copy = pltpu.make_async_copy(lead_ref, work, sem)
    copy.start()
    copy.wait()
    high = lax.Precision.HIGHEST

    def at(i):
        return pl.ds(pl.multiple_of(i * PW, PW), PW)

    def panel(k, carry):
        low = pl.ds(pl.multiple_of(k * PW, TB), TB)
        top = pl.ds(pl.multiple_of(k * PW + TB, TB), TB)
        u1, w1 = chol_inv(work[low, low])
        l21 = dot_nt(work[top, low], w1, high)
        u2, w2 = chol_inv(work[top, top] - dot_nt(l21, l21, high))
        w21 = -dot_nn(w2, dot_nn(l21, w1, high), high)
        work[low, low] = u1.T
        work[low, top] = jnp.zeros((TB, TB), jnp.float32)
        work[top, low] = l21
        work[top, top] = u2.T
        inverse_ref[k, :TB, :TB] = w1
        inverse_ref[k, :TB, TB:] = jnp.zeros((TB, TB), jnp.float32)
        inverse_ref[k, TB:, :TB] = w21
        inverse_ref[k, TB:, TB:] = w2

        def below(i, c):
            solved = dot_nt_split(work[at(i), at(k)], inverse_ref[k])
            work[at(i), at(k)] = solved
            bits_ref[at(i), at(k)] = solved.astype(jnp.bfloat16)
            return c

        lax.fori_loop(k + 1, PANELS, below, 0)

        def column(j, c):
            def row(i, c2):
                work[at(i), at(j)] -= dot_nt(bits_ref[at(i), at(k)], bits_ref[at(j), at(k)])
                return c2

            return lax.fori_loop(j, PANELS, row, c)

        lax.fori_loop(k + 1, PANELS, column, 0)
        return carry

    lax.fori_loop(0, PANELS, panel, 0)
    me = jnp.minimum(me_ref[0], PANELS - 1)

    def out(j, c):
        own_ref[:, at(j)] = jnp.where(j <= me, work[at(me), at(j)], 0.0)
        return c

    lax.fori_loop(0, PANELS, out, 0)


def factor_pivots(me, lead):
    order = PANELS * PW
    return pl.pallas_call(
        pivot_kernel,
        grid_spec=pltpu.PrefetchScalarGridSpec(
            num_scalar_prefetch=1,
            grid=(1,),
            in_specs=[pl.BlockSpec(memory_space=pl.ANY)],
            out_specs=[
                pl.BlockSpec((order, order), lambda i, m: (0, 0)),
                pl.BlockSpec((PANELS, PW, PW), lambda i, m: (0, 0, 0)),
                pl.BlockSpec((PW, order), lambda i, m: (0, 0)),
            ],
            scratch_shapes=[pltpu.VMEM((order, order), jnp.float32), pltpu.SemaphoreType.DMA],
        ),
        out_shape=[
            jax.ShapeDtypeStruct((order, order), jnp.bfloat16),
            jax.ShapeDtypeStruct((PANELS, PW, PW), jnp.float32),
            jax.ShapeDtypeStruct((PW, order), jnp.float32),
        ],
        compiler_params=pltpu.CompilerParams(vmem_limit_bytes=48 * MIB),
        cost_estimate=pl.CostEstimate(
            flops=80_000_000_000, bytes_accessed=20_000_000, transcendentals=0
        ),
        name="factor_pivots",
    )(me, lead)


def pack_kernel(pick_ref, tiles_ref, outbox_ref, sem):
    count = outbox_ref.shape[0]

    def send(i, c):
        pltpu.make_async_copy(tiles_ref.at[pick_ref[i]], outbox_ref.at[i], sem).start()
        return c

    lax.fori_loop(0, count, send, 0)
    pltpu.make_async_copy(outbox_ref, outbox_ref, sem).wait()


def pack_tiles(pick, tiles):
    count = pick.shape[0]
    return pl.pallas_call(
        pack_kernel,
        grid_spec=pltpu.PrefetchScalarGridSpec(
            num_scalar_prefetch=1,
            grid=(1,),
            in_specs=[pl.BlockSpec(tiles.shape, lambda i, p: (0, 0, 0))],
            out_specs=pl.BlockSpec(memory_space=pl.ANY),
            scratch_shapes=[pltpu.SemaphoreType.DMA],
        ),
        out_shape=jax.ShapeDtypeStruct((count, TB, TB), jnp.bfloat16),
        compiler_params=pltpu.CompilerParams(vmem_limit_bytes=32 * MIB),
        name="pack_tiles",
    )(pick, tiles)


CHUNK = 32


def solve_kernel(
    tags_ref, me_ref, front_ref, inbox_ref, bits_ref, inverse_ref, own_ref,
    factor_ref, rows_ref, rest_ref, work, landed, sems, rest_sem,
):
    pivots = PANELS * PW
    count = inbox_ref.shape[0]
    chunks = count // CHUNK
    fill = pltpu.make_async_copy(front_ref, work, sems.at[chunks])
    fill.start()

    def fetch(c):
        part = pl.ds(c * CHUNK, CHUNK)
        return pltpu.make_async_copy(inbox_ref.at[part], landed.at[part], sems.at[c])

    for c in range(chunks):
        fetch(c).start()
    fill.wait()

    for c in range(chunks):
        fetch(c).wait()

        def add(i, carry):
            code = tags_ref[i]

            @pl.when(code >= 0)
            def _():
                place = (
                    pl.ds(pl.multiple_of((code // 64) * TB, TB), TB),
                    pl.ds(pl.multiple_of((code % 64) * TB, TB), TB),
                )
                work[place] += landed[i].astype(jnp.float32)

            return carry

        lax.fori_loop(c * CHUNK, (c + 1) * CHUNK, add, 0)
    leave = pltpu.make_async_copy(work.at[:, pl.ds(pivots, rest_ref.shape[1])], rest_ref, rest_sem)
    leave.start()
    below = me_ref[0] >= PANELS
    for k in range(PANELS):
        at = slice(k * PW, (k + 1) * PW)
        current = work[:, at]
        if k:
            current = current - dot_nt(rows_ref[:, : k * PW], bits_ref[at, : k * PW])
        solved = dot_nt_split(current, inverse_ref[k])
        rows_ref[:, at] = solved.astype(jnp.bfloat16)
        factor_ref[:, at] = jnp.where(below, solved, own_ref[:, at])
    leave.wait()


def solve_rows(tags, me, front, inbox, bits, inverse, own):
    order = front.shape[1]
    pivots = PANELS * PW
    whole = lambda shape: pl.BlockSpec(shape, lambda i, t, m: (0,) * len(shape))
    count = inbox.shape[0]
    return pl.pallas_call(
        solve_kernel,
        grid_spec=pltpu.PrefetchScalarGridSpec(
            num_scalar_prefetch=2,
            grid=(1,),
            in_specs=[
                pl.BlockSpec(memory_space=pl.ANY),
                pl.BlockSpec(memory_space=pl.ANY),
                whole(bits.shape),
                whole(inverse.shape),
                whole(own.shape),
            ],
            out_specs=[
                whole((PW, pivots)),
                whole((PW, pivots)),
                pl.BlockSpec(memory_space=pl.ANY),
            ],
            scratch_shapes=[
                pltpu.VMEM((PW, order), jnp.float32),
                pltpu.VMEM(inbox.shape, jnp.bfloat16),
                pltpu.SemaphoreType.DMA((count // CHUNK + 1,)),
                pltpu.SemaphoreType.DMA,
            ],
        ),
        out_shape=[
            jax.ShapeDtypeStruct((PW, pivots), jnp.float32),
            jax.ShapeDtypeStruct((PW, pivots), jnp.bfloat16),
            jax.ShapeDtypeStruct((PW, order - pivots), jnp.float32),
        ],
        compiler_params=pltpu.CompilerParams(vmem_limit_bytes=56 * MIB),
        name="solve_rows",
    )(tags, me, front, inbox, bits, inverse, own)


def schur_kernel(me_ref, rest_ref, rows_ref, others_ref, out_ref):
    term = dot_nt(rows_ref[...], others_ref[...])
    out_ref[...] = jnp.where(me_ref[0] >= PANELS, rest_ref[...] - term, 0.0)


def schur_rows(me, rest, rows, gathered):
    width = rest.shape[1]
    return pl.pallas_call(
        schur_kernel,
        grid_spec=pltpu.PrefetchScalarGridSpec(
            num_scalar_prefetch=1,
            grid=(width // PW,),
            in_specs=[
                pl.BlockSpec((PW, PW), lambda j, m: (0, j)),
                pl.BlockSpec(rows.shape, lambda j, m: (0, 0)),
                pl.BlockSpec((PW, rows.shape[1]), lambda j, m: (j + PANELS, 0)),
            ],
            out_specs=pl.BlockSpec((PW, PW), lambda j, m: (0, j)),
        ),
        out_shape=jax.ShapeDtypeStruct(rest.shape, jnp.float32),
        compiler_params=pltpu.CompilerParams(vmem_limit_bytes=32 * MIB),
        name="schur_rows",
    )(me, rest, rows, gathered)


def lead_everywhere(work, fronts):
    pivots = PANELS * PW
    share = PW // fronts
    pieces = lax.all_to_all(
        work[:, :pivots].reshape(fronts, share, pivots), "front", 0, 0, tiled=True
    )
    packed = jnp.concatenate(
        [
            jnp.concatenate(
                [pieces[i, :, : (i + 1) * PW], pieces[PANELS - 1 - i, :, : (PANELS - i) * PW]],
                axis=1,
            )
            for i in range(PANELS // 2)
        ],
        axis=0,
    )
    everyone = lax.all_gather(packed, "front", axis=0).reshape(fronts, PANELS // 2, share, -1)
    lead = [None] * PANELS
    for i in range(PANELS // 2):
        both = everyone[:, i].reshape(fronts * share, -1)
        for at, block in ((i, both[:, : (i + 1) * PW]), (PANELS - 1 - i, both[:, (i + 1) * PW :])):
            lead[at] = jnp.pad(block, ((0, 0), (0, pivots - block.shape[1])))
    return jnp.concatenate(lead, axis=0)


def on_device(front_matrix, child_tiles, tile_route, tile_row, tile_col):
    work = front_matrix[0]
    tiles = child_tiles[0]
    count = tiles.shape[0]
    groups = lax.axis_size("group")
    fronts = lax.axis_size("front")
    devices = groups * fronts
    tail = fronts - PANELS
    me = lax.axis_index("front")
    mine = lax.axis_index("group") * fronts + me
    lead = lead_everywhere(work, fronts)

    target = tile_route[0, :, 0]
    destination = target // tail * fronts + PANELS + target % tail
    code = (destination * 2 + tile_row[0]) * 64 + tile_col[0]
    positions = jnp.arange(count, dtype=jnp.int32)
    meets = destination[None, :] == jnp.arange(devices, dtype=jnp.int32)[:, None]
    first = jnp.min(jnp.where(meets, positions[None, :], count), axis=1)
    last = jnp.max(jnp.where(meets, positions[None, :], -1), axis=1)
    pick = jnp.stack([jnp.where(first < count, first, 0), jnp.maximum(last, 0)], axis=1)
    codes = lax.all_gather(code, ("group", "front"), axis=0).reshape(devices, count)
    here = codes // 128 == mine
    from_first = jnp.min(jnp.where(here, positions[None, :], count), axis=1)
    from_last = jnp.max(jnp.where(here, positions[None, :], -1), axis=1)
    label = codes % 128
    tag_first = jnp.max(
        jnp.where(positions[None, :] == from_first[:, None], label, -1), axis=1
    )
    tag_last = jnp.max(
        jnp.where(
            (positions[None, :] == from_last[:, None]) & (from_last != from_first)[:, None],
            label,
            -1,
        ),
        axis=1,
    )
    tags = jnp.stack([tag_first, tag_last], axis=1).reshape(devices * SLOTS)

    outbox = pack_tiles(pick.reshape(devices * SLOTS), tiles)
    inbox = lax.all_to_all(
        outbox.reshape(devices, SLOTS, TB, TB), ("group", "front"), 0, 0, tiled=True
    ).reshape(devices * SLOTS, TB, TB)

    self = me.astype(jnp.int32).reshape(1)
    bits, inverse, own = factor_pivots(self, lead)
    factor, rows, rest = solve_rows(tags, self, work, inbox, bits, inverse, own)
    gathered = lax.all_gather(rows, "front", axis=0, tiled=True)
    schur = schur_rows(self, rest, rows, gathered)
    return (factor[None], schur[None])


def solution(mesh):
    return jax.shard_map(
        on_device,
        mesh=mesh,
        in_specs=(
            P("group", "front", None),
            P("group", "front", None, None),
            P("group", "front", None),
            P("group", "front"),
            P("group", "front"),
        ),
        out_specs=(P("group", "front", None), P("group", "front", None)),
        check_vma=False,
    )
```

time: 1630 us -> 426 us (0.26)
  waiting for transfers between devices: 968 us -> 96.3 us
  other arithmetic: 421 us -> 1.77 us
  blocking collectives: 0 us -> 160 us
  Pallas kernels: 0 us -> 122 us
  local copies, waits for them, and re-layouts: 132 us -> 22.8 us
  matrix products: 55.7 us -> 0 us
    psum x6 -> x0, waiting for transfers between devices: 595 us -> none  [spread(): return lax.psum(jnp.where(mine, x, jnp.zeros_like(x)), axis)]
    another operation x61 -> x2, other arithmetic: 330 us -> 0.02 us  [the longest x1 0.01 us: on_device(): jnp.stack([jnp.where(first < count, first, 0), jnp.maximum(last, 0)], axi...]
    all_gather x6 -> x2, waiting for transfers between devices: 288 us -> 96.3 us  [the longest x1 96.3 us: on_device(): gathered = lax.all_gather(rows, 'front', axis=0, tiled=True)]
    all_gather x0 -> x1, blocking collectives: none -> 129 us  [on_device(): lax.all_gather(code, ('group', 'front'), axis=0).reshape(devices, count)]
    pallas_call x0 -> x4, Pallas kernels: none -> 122 us  [the longest x1 71.4 us: factor_pivots(): pl.pallas_call(pivot_kernel, grid_spec=pltpu.PrefetchScalarGridSpec(num_s...]
    all_to_all x2 -> x1, waiting for transfers between devices: 85.1 us -> 0.01 us  [on_device(): lax.all_to_all(outbox.reshape(devices, SLOTS, TB, TB), ('group', 'front')...]
    scatter-add x1 -> x0, other arithmetic: 54.9 us -> none  [on_device(): blocks.at[tags[:, 0], :, tags[:, 1], :]]
    dot_general x6 -> x0, matrix products: 36.3 us -> none  [contract_rows(): lax.dot_general(left_rows, right_rows, (((1,), (1,)), ((), ())), preferre...]
  transfers between devices with their start and end apart: 14 -> 3, of which waited for: 13 -> 1; matrix products, arithmetic and copies ran while one was open for 3% -> 1% of each run, Pallas kernels for 0% -> 20%
where the time goes in v1:
time: 426 us; the launch traced here: 425 us
  blocking collectives  160 us (38%)
  Pallas kernels  122 us (29%)
  waiting for transfers between devices  96.3 us (23%)
  local copies, waits for them, and re-layouts  22.8 us (5%)
  between operations  14.3 us (3%)
  starting transfers between devices  7.25 us (2%)
    all_gather x1, blocking collectives, on_device(): lax.all_gather(code, ('group', 'front'), axis=0).reshape(devices, count)  129 us
    all_gather x1, waiting for transfers between devices, on_device(): gathered = lax.all_gather(rows, 'front', axis=0, tiled=True)  96.3 us
    pallas_call x1, Pallas kernels, factor_pivots(): pl.pallas_call(pivot_kernel, grid_spec=pltpu.PrefetchScalarGridSpec(num_s...  71.4 us
    all_to_all x1, blocking collectives, lead_everywhere(): lax.all_to_all(work[:, :pivots].reshape(fronts, share, pivots), 'front',...  31.2 us
    pallas_call x1, Pallas kernels, schur_rows(): pl.pallas_call(schur_kernel, grid_spec=pltpu.PrefetchScalarGridSpec(num_s...  23.4 us
    unnamed x28, local copies, waits for them, and re-layouts  16.9 us
    pallas_call x1, Pallas kernels, solve_rows(): pl.pallas_call(solve_kernel, grid_spec=pltpu.PrefetchScalarGridSpec(num_s...  14.1 us
    pallas_call x1, Pallas kernels, pack_tiles(): pl.pallas_call(pack_kernel, grid_spec=pltpu.PrefetchScalarGridSpec(num_sc...  13.5 us
  transfers between devices with their start and end apart: 3, of which 1 were waited for; matrix products, arithmetic and copies ran while one was open for 1% of the time, Pallas kernels for 20%

profile of v1, /device:TPU:1, one launch (start us, length us, event | category | flops | bytes accessed | tf_op | source)
XLA Modules:
  0.0 424.7 jit_solution(1242535992446728303)
XLA Ops:
  7.2 0.0 all-gather.7.cloned.1.call-start
  7.2 1.5 slice_bitcast_fusion.3
  8.7 0.0 copy-start.12
  8.7 31.2 %all_to_all.10 = f32[32,8,1536]{2,1,0:T(8,128)S(1)} all-to-all(f32[32,8,1536]{2,1,0:T(8,128)S(1)} %slice_bitcast_fusion.3), channel_id=1, replica_groups=mesh['group'=4,'front'=32] {'front'}, dimensions={0} | all-to-all | bytes 3145728 | tf_op jit(solution)/shard_map/all_to_all | solution.py:340
  40.0 0.7 maximum_maximum_fusion
  40.7 0.0 all-gather.7.cloned.1.call-update
  40.7 0.0 copy-done.12
  40.7 0.1 select_reduce_fusion.1
  40.9 0.1 copy.16
  41.0 0.1 reshape.141.pick_ref
  41.1 0.0 copy-start.2
  41.1 2.2 copy-done.2
  43.3 13.5 %pack_tiles.1 = bf16[256,128,128]{2,1,0:T(8,128)(2,1)S(1)} custom-call(s32[256]{0:T(256)S(1)} %reshape.141.pick_ref, bf16[128,128,128]{2,1,0:T(8,128)(2,1)S(1)} %bitcast.76), custom_call_target="tpu_custom_call" | custom-call | tf_op jit(solution)/shard_map/pack_tiles/pallas_call | solution.py:206
  56.8 0.0 copy-start
  56.8 3.3 copy-done
  60.1 0.0 copy-start.10
  60.1 0.0 copy-start.11
  60.1 7.2 %all-to-all-start = ((bf16[128,2,128,128]{3,2,1,0:T(8,128)(2,1)}), bf16[128,2,128,128]{3,2,1,0:T(8,128)(2,1)}, u32[]{:S(2)}, u32[]{:S(2)}) async-start(bf16[128,2,128,128]{3,2,1,0:T(8,128)(2,1)} %bitcast.75), calls=%async_computation | async-start | bytes 16777216 | tf_op jit(solution)/shard_map/all_to_all | solution.py:401
  67.3 0.0 all-gather.5.cloned.1.call-start
  67.4 0.0 copy-done.10
  67.4 0.0 copy-done.11
  67.4 128.7 %all-gather.1 = s32[128,1,128]{2,1,0:T(1,128)S(1)} all-gather(s32[1,1,128]{2,1,0:T(1,128)S(1)} %add_bitcast_fusion), channel_id=1, replica_groups=mesh['group'=4,'front'=32] {'group','front'}, dimensions={0}, use_global_device_ids=true | all-gather | bytes 66048 | tf_op jit(solution)/shard_map/all_gather | solution.py:382
  196.1 0.1 select_reduce_fusion.5
  196.2 0.2 select_reduce_fusion.4
  196.5 0.1 copy.15
  196.6 0.7 reshape.139.tags_ref
  197.3 0.0 all-gather.7.cloned.1.call-done
  197.3 3.0 slice_bitcast_fusion
  200.3 0.1 slice.80
  200.4 0.0 copy-start.9
  200.4 0.1 slice.81
  200.5 0.0 copy-start.8
  200.5 0.6 copy-done.9
  201.1 0.2 fusion.2
  201.3 0.0 copy-done.8
  201.3 0.0 copy-start.7
  201.3 0.2 fusion.1
  201.5 0.5 copy-done.7
  202.0 0.2 fusion
  202.2 0.2 pad_dynamic-update-slice_fusion.1
  202.3 0.2 pad_dynamic-update-slice_fusion
  202.5 0.2 slice_dynamic-update-slice_fusion.lead_ref
  202.7 0.0 copy-start.6
  202.7 3.6 copy-done.6
  206.4 71.4 %factor_pivots.1 = (bf16[1536,1536]{1,0:T(8,128)(2,1)}, f32[6,256,256]{2,1,0:T(8,128)S(1)}, f32[256,1536]{1,0:T(8,128)S(1)}) custom-call(s32[1]{0:T(128)} %bitcast.7.me_ref, f32[1536,1536]{1,0:T(8,128)} %copy-done.6), custom_call_target="tpu_custom_call" | custom-call | flops 80000000000 | bytes 20000000 | tf_op jit(solution)/shard_map/factor_pivots/pallas_call | solution.py:167
  277.7 0.0 copy-start.4
  277.8 1.1 copy-done.4
  278.9 0.0 copy-start.5
  278.9 1.1 copy-done.5
  280.0 0.0 all-to-all-done
  280.0 14.1 %solve_rows.1 = (f32[256,1536]{1,0:T(8,128)}, bf16[256,1536]{1,0:T(8,128)(2,1)}, f32[256,6656]{1,0:T(8,128)}) custom-call(s32[256]{0:T(256)} %reshape.139.tags_ref, s32[1]{0:T(128)} %bitcast.7.me_ref, f32[256,8192]{1,0:T(8,128)} %bitcast.78, bf16[256,128,128]{2,1,0:T(8,128)(2,1)} %bitcast.16.inbox_ref, bf16[1536,1536]{1,0:T(8,128)(2,1)} %get-tuple-element.8.bits_ref, ...), custom_call_target="tpu_custom_call" | custom-call | tf_op jit(solution)/shard_map/solve_rows/pallas_call | solution.py:278
  294.1 0.0 all-gather.5.cloned.1.call-update
  294.1 96.3 %all-gather.5.cloned.1.call-done.others_ref = bf16[8192,1536]{1,0:T(8,128)(2,1)} async-done(((bf16[256,1536]{1,0:T(8,128)(2,1)}), bf16[8192,1536]{1,0:T(8,128)(2,1)}) %all-gather.5.cloned.1.call-update) | async-done | bytes 25165840 | tf_op jit(solution)/shard_map/all_gather | solution.py:408
  390.4 0.0 copy-start.1
  390.4 2.9 copy-done.1
  393.3 0.0 copy-start.3
  393.3 1.1 copy-done.3
  394.5 23.4 %schur_rows.1 = f32[256,6656]{1,0:T(8,128)} custom-call(s32[1]{0:T(128)} %bitcast.7.me_ref, f32[256,6656]{1,0:T(8,128)S(1)} %copy-done.1, bf16[256,1536]{1,0:T(8,128)(2,1)S(1)} %copy-done.3, bf16[8192,1536]{1,0:T(8,128)(2,1)} %all-gather.5.cloned.1.call-done.others_ref), custom_call_target="tpu_custom_call" | custom-call | tf_op jit(solution)/shard_map/schur_rows/pallas_call | solution.py:319
  (13 shorter events, 0.1 us)
Async XLA Ops:
  7.2 190.2 %all-gather.7.cloned.1.call-start = ((), (), s32[]{:S(2)}) async-start(), calls=%async_computation.3 | async-start | bytes 5677056 | tf_op jit(solution)/shard_map/all_gather | solution.py:353
  8.7 32.0 %copy-start.12 = (s32[1,128,1]{1,2,0:T(1,128)S(1)}, s32[1,128,1]{1,2,0:T(1,128)}, u32[]{:S(2)}) copy-start(s32[1,128,1]{1,2,0:T(1,128)} %param.7) | copy-start | bytes 1540
  41.1 2.2 copy-start.2
  56.8 3.3 copy-start
  60.1 7.2 %copy-start.10 = (s32[1,128]{1,0:T(1,128)S(1)}, s32[1,128]{1,0:T(1,128)}, u32[]{:S(2)}) copy-start(s32[1,128]{1,0:T(1,128)} %param.9) | copy-start | bytes 1540
  60.1 7.2 %copy-start.11 = (s32[1,128]{1,0:T(1,128)S(1)}, s32[1,128]{1,0:T(1,128)}, u32[]{:S(2)}) copy-start(s32[1,128]{1,0:T(1,128)} %param.8) | copy-start | bytes 1540
  60.1 219.9 %all-to-all-start = ((bf16[128,2,128,128]{3,2,1,0:T(8,128)(2,1)}), bf16[128,2,128,128]{3,2,1,0:T(8,128)(2,1)}, u32[]{:S(2)}, u32[]{:S(2)}) async-start(bf16[128,2,128,128]{3,2,1,0:T(8,128)(2,1)} %bitcast.75), calls=%async_computation | async-start | bytes 16777216 | tf_op jit(solution)/shard_map/all_to_all | solution.py:401
  67.3 323.1 %all-gather.5.cloned.1.call-start = ((), (), s32[]{:S(2)}) async-start(), calls=%async_computation.2 | async-start | bytes 25952256 | tf_op jit(solution)/shard_map/all_gather | solution.py:408
  200.4 0.7 copy-start.9
  200.5 0.8 copy-start.8
  201.3 0.7 copy-start.7
  202.7 3.6 copy-start.6
  277.7 1.1 copy-start.4
  278.9 1.1 copy-start.5
  390.4 2.9 copy-start.1
  393.3 1.1 copy-start.3
Sparse Core Ops, SparseCore 0:
  40.8 117.9 all-gather.6
  294.3 96.1 all-gather.4

commit v2 on v1

--- a/solution.py
+++ b/solution.py
@@ -109,42 +109,345 @@
     return jnp.concatenate(upper, axis=0), jnp.concatenate(inverse, axis=0)
 
 
-def pivot_kernel(me_ref, lead_ref, bits_ref, inverse_ref, own_ref, work, sem):
-    copy = pltpu.make_async_copy(lead_ref, work, sem)
-    copy.start()
-    copy.wait()
+def share_segments(i):
+    half_width = (PANELS + 1) * PW // 2
+    group = min(i, PANELS - 1 - i)
+    begin = 0 if i < PANELS // 2 else (group + 1) * PW
+    end = begin + (i + 1) * PW
+    found = []
+    for half in range(2):
+        low, high = max(begin, half * half_width), min(end, (half + 1) * half_width)
+        if low < high:
+            found.append((half, group, low - half * half_width, low - begin, high - low))
+    return found
+
+
+MESH = pl.DeviceIdType.MESH
+SIDE = 4
+SENDS = 64
+MOVES = {"b+": (0, 3), "b-": (0, 1), "a+": (3, 0), "a-": (1, 0)}
+
+
+def when(condition, action):
+    if condition is None:
+        action()
+    else:
+        pl.when(condition)(action)
+
+
+class Ring:
+    def __init__(self, skip):
+        me = lax.axis_index("front")
+        self.me = me
+        self.core = me % 2
+        x, y = (me // 2) % SIDE, me // (2 * SIDE)
+        self.a = jnp.where(self.core == 0, y, x)
+        self.b = jnp.where(self.core == 0, x, y)
+        self.skip = skip
+        self.sends = 0
+        self.late = []
+        self.peer = {"s": me + 1 - 2 * self.core}
+        for name, (da, db) in MOVES.items():
+            self.peer[name] = 2 * self.chip(SIDE - da, SIDE - db) + self.core
+
+    def chip(self, da, db, other=False):
+        core = 1 - self.core if other else self.core
+        a, b = (self.b, self.a) if other else (self.a, self.b)
+        a, b = (a + da) % SIDE, (b + db) % SIDE
+        return jnp.where(core == 0, a * SIDE + b, b * SIDE + a)
+
+    def live(self, da, db, other=False):
+        return self.chip(da, db, other) * 2 >= self.skip if self.skip else None
+
+    def greet(self):
+        barrier = pltpu.get_barrier_semaphore()
+        for peer in self.peer.values():
+            pl.semaphore_signal(barrier, inc=1, device_id={"front": peer}, device_id_type=MESH)
+        return barrier
+
+    def gather(self, own, out, ring_recv, side_recv, own_recv, local_sem, send_sem):
+        core = self.core
+
+        def piece(da, db, s, other=False):
+            half = 1 - core if other else core
+            chip = self.chip(da, db, other)
+            if s is None:
+                return out.at[pl.ds(2 * chip, 2), half]
+            return out.at[2 * chip + s, half]
+
+        def remote(source, target, recv, to, condition):
+            k = self.sends
+            self.sends += 1
+
+            def make():
+                return pltpu.make_async_remote_copy(
+                    src_ref=source,
+                    dst_ref=target,
+                    send_sem=send_sem.at[k],
+                    recv_sem=recv,
+                    device_id={"front": self.peer[to]},
+                    device_id_type=MESH,
+                )
+
+            when(condition, lambda: make().start())
+            self.late.append((condition, lambda: make().wait_send()))
+
+        def arrive(ref, sem, condition):
+            def wait():
+                pltpu.make_async_remote_copy(
+                    src_ref=ref,
+                    dst_ref=ref,
+                    send_sem=send_sem.at[0],
+                    recv_sem=sem,
+                    device_id={"front": self.peer["s"]},
+                    device_id_type=MESH,
+                ).wait_recv()
+
+            when(condition, wait)
+
+        def give(da, db, s, to):
+            ref = piece(da, db, s)
+            at = 0 if s is None else s
+            if to == "s":
+                recv = side_recv.at[da, db, at]
+            else:
+                recv = ring_recv.at[(da + MOVES[to][0]) % SIDE, (db + MOVES[to][1]) % SIDE, at]
+            remote(ref, ref, recv, to, self.live(da, db))
+
+        here = self.live(0, 0)
+        mine = pltpu.make_async_copy(own(core), piece(0, 0, core), local_sem.at[0])
+        rest = pltpu.make_async_copy(own(1 - core), piece(0, 0, core, True), local_sem.at[1])
+        when(here, mine.start)
+        when(here, rest.start)
+        remote(own(1 - core), piece(0, 0, core, True), own_recv.at[0], "s", here)
+        remote(own(core), piece(0, 0, core), own_recv.at[1], "s", here)
+        when(here, mine.wait)
+        arrive(piece(0, 0, 1 - core), own_recv.at[0], here)
+        for to in MOVES:
+            give(0, 0, None, to)
+        steps = [
+            (0, 3, None, [(0, "b+"), (None, "a+"), (None, "a-")]),
+            (0, 1, None, [(1, "b-"), (None, "a+"), (None, "a-")]),
+            (3, 0, None, [(0, "a+")]),
+            (1, 0, None, [(1, "a-")]),
+            (0, 2, 0, [(0, "a+"), (0, "a-")]),
+            (0, 2, 1, [(1, "a+"), (1, "a-")]),
+            (3, 3, None, [(0, "a+")]),
+            (1, 3, None, [(1, "a-")]),
+            (3, 1, None, [(0, "a+")]),
+            (1, 1, None, [(1, "a-")]),
+            (2, 0, 0, []),
+            (2, 0, 1, []),
+            (3, 2, 0, [(0, "a+")]),
+            (1, 2, 1, [(1, "a-")]),
+            (3, 2, 1, []),
+            (1, 2, 0, []),
+            (2, 3, 0, []),
+            (2, 3, 1, []),
+            (2, 1, 0, []),
+            (2, 1, 1, []),
+            (2, 2, 0, []),
+            (2, 2, 1, []),
+        ]
+        for da, db, s, onward in steps:
+            arrive(piece(da, db, s), ring_recv.at[da, db, s or 0], self.live(da, db))
+            for part, to in onward:
+                give(da, db, part, to)
+            give(da, db, s, "s")
+        arrive(piece(0, 0, 1 - core, True), own_recv.at[1], here)
+        when(here, rest.wait)
+        for da, db, s, _ in steps:
+            arrive(piece(da, db, s, True), side_recv.at[da, db, s or 0], self.live(da, db, True))
+        for condition, wait in self.late:
+            when(condition, wait)
+
+
+RING_SEMS = [
+    pltpu.SemaphoreType.DMA((SIDE, SIDE, 2)),
+    pltpu.SemaphoreType.DMA((SIDE, SIDE, 2)),
+    pltpu.SemaphoreType.DMA((2,)),
+    pltpu.SemaphoreType.DMA((2,)),
+    pltpu.SemaphoreType.DMA((SENDS,)),
+]
+
+
+def gather_kernel(rows_ref, out_ref, *sems):
+    ring = Ring(PANELS)
+    pl.semaphore_wait(ring.greet(), len(ring.peer))
+    ring.gather(lambda h: rows_ref.at[h], out_ref, *sems)
+
+
+def gather_rows(rows):
+    fronts = lax.axis_size("front")
+    halved = rows.reshape(2, rows.shape[0] // 2, rows.shape[1])
+    out = pl.pallas_call(
+        gather_kernel,
+        in_specs=[pl.BlockSpec(memory_space=pl.ANY)],
+        out_specs=pl.BlockSpec(memory_space=pl.ANY),
+        out_shape=jax.ShapeDtypeStruct((fronts,) + halved.shape, rows.dtype),
+        scratch_shapes=RING_SEMS,
+        compiler_params=pltpu.CompilerParams(collective_id=1, has_side_effects=True),
+        name="gather_rows",
+    )(halved)
+    return out.reshape(fronts * rows.shape[0], rows.shape[1])
+
+
+def spread_kernel(front_ref, out_ref, share, deal_recv, deal_send, *sems):
+    fronts = out_ref.shape[0]
+    ring = Ring(0)
+    me = ring.me
+    barrier = ring.greet()
+    for i in range(PANELS):
+
+        @pl.when(me != i)
+        def _():
+            pl.semaphore_signal(barrier, inc=1, device_id={"front": i}, device_id_type=MESH)
+
+    @pl.when(me < PANELS)
+    def _():
+        pl.semaphore_wait(barrier, len(ring.peer) + fronts - 1)
+
+    @pl.when(me >= PANELS)
+    def _():
+        pl.semaphore_wait(barrier, len(ring.peer))
+
+    pieces = []
+    for i in range(PANELS):
+        for segment in share_segments(i):
+            pieces.append((i, len(pieces)) + segment)
+
+    def source(f, piece):
+        i, _, _, _, _, column, width = piece
+        return front_ref.at[pl.ds(pl.multiple_of(f * 8, 8), 8), pl.ds(column, width)]
+
+    def target(piece):
+        _, _, half, group, column, _, width = piece
+        return share.at[half, pl.ds(group * 8, 8), pl.ds(column, width)]
+
+    def far(f, piece):
+        return pltpu.make_async_remote_copy(
+            src_ref=source(f, piece),
+            dst_ref=target(piece),
+            send_sem=deal_send.at[piece[2], f],
+            recv_sem=deal_recv.at[piece[1]],
+            device_id={"front": f},
+            device_id_type=MESH,
+        )
+
+    def near(piece):
+        return pltpu.make_async_copy(source(me, piece), target(piece), deal_recv.at[piece[1]])
+
+    for i in range(PANELS):
+        mine = [piece for piece in pieces if piece[0] == i]
+
+        @pl.when(me == i)
+        def _():
+            def deal(f, c):
+                @pl.when(f != me)
+                def _():
+                    for piece in mine:
+                        far(f, piece).start()
+
+                return c
+
+            lax.fori_loop(0, fronts, deal, 0)
+            for piece in mine:
+                near(piece).start()
+
+    for piece in pieces:
+
+        @pl.when(me == piece[0])
+        def _():
+            near(piece).wait()
+
+        @pl.when(me != piece[0])
+        def _():
+            far(0, piece).wait_recv()
+
+    ring.gather(lambda h: share.at[h], out_ref, *sems)
+    for i in range(PANELS):
+        mine = [piece for piece in pieces if piece[0] == i]
+
+        @pl.when(me == i)
+        def _():
+            def done(f, c):
+                @pl.when(f != me)
+                def _():
+                    for piece in mine:
+                        far(f, piece).wait_send()
+
+                return c
+
+            lax.fori_loop(0, fronts, done, 0)
+
+
+def spread_pivots(front):
+    fronts = lax.axis_size("front")
+    share = (2, PANELS // 2 * (PW // fronts), (PANELS + 1) * PW // 2)
+    return pl.pallas_call(
+        spread_kernel,
+        in_specs=[pl.BlockSpec(memory_space=pl.ANY)],
+        out_specs=pl.BlockSpec(memory_space=pl.ANY),
+        out_shape=jax.ShapeDtypeStruct((fronts,) + share, jnp.float32),
+        scratch_shapes=[
+            pltpu.VMEM(share, jnp.float32),
+            pltpu.SemaphoreType.DMA((9,)),
+            pltpu.SemaphoreType.DMA((2, fronts)),
+        ]
+        + RING_SEMS,
+        compiler_params=pltpu.CompilerParams(collective_id=2, has_side_effects=True),
+        name="spread_pivots",
+    )(front)
+
+
+def pivot_kernel(me_ref, shares_ref, bits_ref, inverse_ref, own_ref, work, sem):
     high = lax.Precision.HIGHEST
-
-    def at(i):
+    fronts = shares_ref.shape[0]
+    for i in range(PANELS):
+        for half, group, source, target, width in share_segments(i):
+            pltpu.make_async_copy(
+                shares_ref.at[:, half, pl.ds(group * 8, 8), pl.ds(source, width)],
+                work.at[pl.ds(i * fronts, fronts), :, pl.ds(target, width)],
+                sem,
+            ).start()
+    pltpu.make_async_copy(shares_ref, shares_ref, sem).wait()
+
+    def cols(i):
         return pl.ds(pl.multiple_of(i * PW, PW), PW)
 
+    def load(i, j):
+        return work[pl.ds(i * 32, 32), :, cols(j)].reshape(PW, PW)
+
     def panel(k, carry):
-        low = pl.ds(pl.multiple_of(k * PW, TB), TB)
-        top = pl.ds(pl.multiple_of(k * PW + TB, TB), TB)
-        u1, w1 = chol_inv(work[low, low])
-        l21 = dot_nt(work[top, low], w1, high)
-        u2, w2 = chol_inv(work[top, top] - dot_nt(l21, l21, high))
+        top = pl.ds(k * 32, 16)
+        low = pl.ds(k * 32 + 16, 16)
+        left = pl.ds(pl.multiple_of(k * PW, TB), TB)
+        right = pl.ds(pl.multiple_of(k * PW + TB, TB), TB)
+        u1, w1 = chol_inv(work[top, :, left].reshape(TB, TB))
+        l21 = dot_nt(work[low, :, left].reshape(TB, TB), w1, high)
+        u2, w2 = chol_inv(work[low, :, right].reshape(TB, TB) - dot_nt(l21, l21, high))
         w21 = -dot_nn(w2, dot_nn(l21, w1, high), high)
-        work[low, low] = u1.T
-        work[low, top] = jnp.zeros((TB, TB), jnp.float32)
-        work[top, low] = l21
-        work[top, top] = u2.T
+        work[top, :, left] = u1.T.reshape(16, 8, TB)
+        work[top, :, right] = jnp.zeros((16, 8, TB), jnp.float32)
+        work[low, :, left] = l21.reshape(16, 8, TB)
+        work[low, :, right] = u2.T.reshape(16, 8, TB)
         inverse_ref[k, :TB, :TB] = w1
         inverse_ref[k, :TB, TB:] = jnp.zeros((TB, TB), jnp.float32)
         inverse_ref[k, TB:, :TB] = w21
         inverse_ref[k, TB:, TB:] = w2
 
         def below(i, c):
-            solved = dot_nt_split(work[at(i), at(k)], inverse_ref[k])
-            work[at(i), at(k)] = solved
-            bits_ref[at(i), at(k)] = solved.astype(jnp.bfloat16)
+            solved = dot_nt_split(load(i, k), inverse_ref[k])
+            work[pl.ds(i * 32, 32), :, cols(k)] = solved.reshape(32, 8, PW)
+            bits_ref[cols(i), cols(k)] = solved.astype(jnp.bfloat16)
             return c
 
         lax.fori_loop(k + 1, PANELS, below, 0)
 
         def column(j, c):
             def row(i, c2):
-                work[at(i), at(j)] -= dot_nt(bits_ref[at(i), at(k)], bits_ref[at(j), at(k)])
+                term = dot_nt(bits_ref[cols(i), cols(k)], bits_ref[cols(j), cols(k)])
+                work[pl.ds(i * 32, 32), :, cols(j)] -= term.reshape(32, 8, PW)
                 return c2
 
             return lax.fori_loop(j, PANELS, row, c)
@@ -156,13 +459,13 @@
     me = jnp.minimum(me_ref[0], PANELS - 1)
 
     def out(j, c):
-        own_ref[:, at(j)] = jnp.where(j <= me, work[at(me), at(j)], 0.0)
+        own_ref[:, cols(j)] = jnp.where(j <= me, load(me, j), 0.0)
         return c
 
     lax.fori_loop(0, PANELS, out, 0)
 
 
-def factor_pivots(me, lead):
+def factor_pivots(me, shares):
     order = PANELS * PW
     return pl.pallas_call(
         pivot_kernel,
@@ -175,7 +478,10 @@
                 pl.BlockSpec((PANELS, PW, PW), lambda i, m: (0, 0, 0)),
                 pl.BlockSpec((PW, order), lambda i, m: (0, 0)),
             ],
-            scratch_shapes=[pltpu.VMEM((order, order), jnp.float32), pltpu.SemaphoreType.DMA],
+            scratch_shapes=[
+                pltpu.VMEM((order // 8, 8, order), jnp.float32),
+                pltpu.SemaphoreType.DMA,
+            ],
         ),
         out_shape=[
             jax.ShapeDtypeStruct((order, order), jnp.bfloat16),
@@ -187,7 +493,7 @@
             flops=80_000_000_000, bytes_accessed=20_000_000, transcendentals=0
         ),
         name="factor_pivots",
-    )(me, lead)
+    )(me, shares)
 
 
 def pack_kernel(pick_ref, tiles_ref, outbox_ref, sem):
@@ -197,7 +503,7 @@
         pltpu.make_async_copy(tiles_ref.at[pick_ref[i]], outbox_ref.at[i], sem).start()
         return c
 
-    lax.fori_loop(0, count, send, 0)
+    lax.fori_loop(0, count, send, 0, unroll=8)
     pltpu.make_async_copy(outbox_ref, outbox_ref, sem).wait()
 
 
@@ -334,31 +640,6 @@
     )(me, rest, rows, gathered)
 
 
-def lead_everywhere(work, fronts):
-    pivots = PANELS * PW
-    share = PW // fronts
-    pieces = lax.all_to_all(
-        work[:, :pivots].reshape(fronts, share, pivots), "front", 0, 0, tiled=True
-    )
-    packed = jnp.concatenate(
-        [
-            jnp.concatenate(
-                [pieces[i, :, : (i + 1) * PW], pieces[PANELS - 1 - i, :, : (PANELS - i) * PW]],
-                axis=1,
-            )
-            for i in range(PANELS // 2)
-        ],
-        axis=0,
-    )
-    everyone = lax.all_gather(packed, "front", axis=0).reshape(fronts, PANELS // 2, share, -1)
-    lead = [None] * PANELS
-    for i in range(PANELS // 2):
-        both = everyone[:, i].reshape(fronts * share, -1)
-        for at, block in ((i, both[:, : (i + 1) * PW]), (PANELS - 1 - i, both[:, (i + 1) * PW :])):
-            lead[at] = jnp.pad(block, ((0, 0), (0, pivots - block.shape[1])))
-    return jnp.concatenate(lead, axis=0)
-
-
 def on_device(front_matrix, child_tiles, tile_route, tile_row, tile_col):
     work = front_matrix[0]
     tiles = child_tiles[0]
@@ -369,7 +650,7 @@
     tail = fronts - PANELS
     me = lax.axis_index("front")
     mine = lax.axis_index("group") * fronts + me
-    lead = lead_everywhere(work, fronts)
+    shares = spread_pivots(work)
 
     target = tile_route[0, :, 0]
     destination = target // tail * fronts + PANELS + target % tail
@@ -403,9 +684,9 @@
     ).reshape(devices * SLOTS, TB, TB)
 
     self = me.astype(jnp.int32).reshape(1)
-    bits, inverse, own = factor_pivots(self, lead)
+    bits, inverse, own = factor_pivots(self, shares)
     factor, rows, rest = solve_rows(tags, self, work, inbox, bits, inverse, own)
-    gathered = lax.all_gather(rows, "front", axis=0, tiled=True)
+    gathered = gather_rows(rows)
     schur = schur_rows(self, rest, rows, gathered)
     return (factor[None], schur[None])
 

time: 426 us -> 411 us (0.965)
  Pallas kernels: 122 us -> 258 us
  waiting for transfers between devices: 96.3 us -> 0.01 us
  blocking collectives: 160 us -> 127 us
  between operations: 14.3 us -> 0.8 us
  local copies, waits for them, and re-layouts: 22.8 us -> 11.7 us
  starting transfers between devices: 7.25 us -> 12 us
    pallas_call x0 -> x2, Pallas kernels: none -> 138 us  [the longest x1 91.3 us: gather_rows(): pl.pallas_call(gather_kernel, in_specs=[pl.BlockSpec(memory_space=pl.ANY)...]
    all_gather x2 -> x0, waiting for transfers between devices: 96.3 us -> none  [the longest x1 96.3 us: on_device(): gathered = lax.all_gather(rows, 'front', axis=0, tiled=True)]
    all_to_all x1 -> x0, blocking collectives: 31.2 us -> none  [lead_everywhere(): lax.all_to_all(work[:, :pivots].reshape(fronts, share, pivots), 'front',...]
    unnamed x28 -> x18, local copies, waits for them, and re-layouts: 16.9 us -> 10.6 us
    all_to_all x1, starting transfers between devices: 7.17 us -> 12 us  [on_device(): lax.all_to_all(outbox.reshape(devices, SLOTS, TB, TB), ('group', 'front')...]
  transfers between devices with their start and end apart: 3 -> 1, of which waited for: 1 -> 0; matrix products, arithmetic and copies ran while one was open for 1% -> 0% of each run, Pallas kernels for 20% -> 28%
where the time goes in v2:
time: 411 us
  Pallas kernels  258 us (63%)
  blocking collectives  127 us (31%)
  starting transfers between devices  12 us (3%)
  local copies, waits for them, and re-layouts  11.7 us (3%)
    all_gather x1, blocking collectives, on_device(): lax.all_gather(code, ('group', 'front'), axis=0).reshape(devices, count)  127 us
    pallas_call x1, Pallas kernels, gather_rows(): pl.pallas_call(gather_kernel, in_specs=[pl.BlockSpec(memory_space=pl.ANY)...  91.3 us
    pallas_call x1, Pallas kernels, factor_pivots(): pl.pallas_call(pivot_kernel, grid_spec=pltpu.PrefetchScalarGridSpec(num_s...  70.2 us
    pallas_call x1, Pallas kernels, spread_pivots(): pl.pallas_call(spread_kernel, in_specs=[pl.BlockSpec(memory_space=pl.ANY)...  46.6 us
    pallas_call x1, Pallas kernels, schur_rows(): pl.pallas_call(schur_kernel, grid_spec=pltpu.PrefetchScalarGridSpec(num_s...  23.5 us
    pallas_call x1, Pallas kernels, solve_rows(): pl.pallas_call(solve_kernel, grid_spec=pltpu.PrefetchScalarGridSpec(num_s...  14 us
    pallas_call x1, Pallas kernels, pack_tiles(): pl.pallas_call(pack_kernel, grid_spec=pltpu.PrefetchScalarGridSpec(num_sc...  12.5 us
    all_to_all x1, starting transfers between devices, on_device(): lax.all_to_all(outbox.reshape(devices, SLOTS, TB, TB), ('group', 'front')...  12 us
  transfers between devices with their start and end apart: 1, of which 0 were waited for; matrix products, arithmetic and copies ran while one was open for 0% of the time, Pallas kernels for 28%

profile of v2, /device:TPU:1, one launch (start us, length us, event | category | flops | bytes accessed | tf_op | source)
XLA Modules:
  0.0 410.6 jit_solution(16619511377073899167)
XLA Ops:
  0.6 0.7 fusion.7
  1.3 0.1 select_reduce_fusion.1
  1.5 0.1 copy.10
  1.6 0.1 reshape.141.pick_ref
  1.7 0.0 copy-start.2
  1.7 2.2 copy-done.2
  3.9 12.5 %pack_tiles.1 = bf16[256,128,128]{2,1,0:T(8,128)(2,1)S(1)} custom-call(s32[256]{0:T(256)S(1)} %reshape.141.pick_ref, bf16[128,128,128]{2,1,0:T(8,128)(2,1)S(1)} %bitcast.51), custom_call_target="tpu_custom_call" | custom-call | tf_op jit(solution)/shard_map/pack_tiles/pallas_call | solution.py:512
  16.5 0.0 copy-start
  16.5 3.2 copy-done
  19.7 0.0 copy-start.6
  19.7 0.0 copy-start.7
  19.7 0.0 copy-start.8
  19.7 12.0 %all-to-all-start = ((bf16[128,2,128,128]{3,2,1,0:T(8,128)(2,1)}), bf16[128,2,128,128]{3,2,1,0:T(8,128)(2,1)}, u32[]{:S(2)}, u32[]{:S(2)}) async-start(bf16[128,2,128,128]{3,2,1,0:T(8,128)(2,1)} %bitcast.50), calls=%async_computation | async-start | bytes 16777216 | tf_op jit(solution)/shard_map/all_to_all | solution.py:682
  31.6 0.0 copy-done.6
  31.7 0.0 copy-done.7
  31.7 0.0 copy-done.8
  31.7 126.8 %all-gather = s32[128,1,128]{2,1,0:T(1,128)S(1)} all-gather(s32[1,1,128]{2,1,0:T(1,128)S(1)} %add_bitcast_fusion), channel_id=1, replica_groups=mesh['group'=4,'front'=32] {'group','front'}, dimensions={0}, use_global_device_ids=true | all-gather | bytes 66048 | tf_op jit(solution)/shard_map/all_gather | solution.py:663
  158.5 0.1 select_reduce_fusion.5
  158.7 0.2 select_reduce_fusion.4
  158.9 0.1 copy.9
  159.0 0.7 reshape.139.tags_ref
  159.7 46.6 %spread_pivots.1.shares_ref = f32[32,2,24,896]{3,2,1,0:T(8,128)} custom-call(f32[256,8192]{1,0:T(8,128)} %bitcast.54), custom_call_target="tpu_custom_call" | custom-call | tf_op jit(solution)/shard_map/spread_pivots/pallas_call | solution.py:387
  206.3 70.2 %factor_pivots.1 = (bf16[1536,1536]{1,0:T(8,128)(2,1)}, f32[6,256,256]{2,1,0:T(8,128)S(1)}, f32[256,1536]{1,0:T(8,128)S(1)}) custom-call(s32[1]{0:T(128)} %bitcast.7.me_ref, f32[32,2,24,896]{3,2,1,0:T(8,128)} %spread_pivots.1.shares_ref), custom_call_target="tpu_custom_call" | custom-call | flops 80000000000 | bytes 20000000 | tf_op jit(solution)/shard_map/factor_pivots/pallas_call | solution.py:470
  276.5 0.0 copy-start.4
  276.5 1.1 copy-done.4
  277.7 0.0 copy-start.5
  277.7 1.1 copy-done.5
  278.8 0.0 all-to-all-done
  278.8 14.0 %solve_rows.1 = (f32[256,1536]{1,0:T(8,128)}, bf16[256,1536]{1,0:T(8,128)(2,1)}, f32[256,6656]{1,0:T(8,128)}) custom-call(s32[256]{0:T(256)} %reshape.139.tags_ref, s32[1]{0:T(128)} %bitcast.7.me_ref, f32[256,8192]{1,0:T(8,128)} %bitcast.55, bf16[256,128,128]{2,1,0:T(8,128)(2,1)} %bitcast.16.inbox_ref, bf16[1536,1536]{1,0:T(8,128)(2,1)} %get-tuple-element.8.bits_ref, ...), custom_call_target="tpu_custom_call" | custom-call | tf_op jit(solution)/shard_map/solve_rows/pallas_call | solution.py:584
  292.8 0.0 copy-start.3
  292.8 91.3 %gather_rows.1 = bf16[32,2,128,1536]{3,2,1,0:T(8,128)(2,1)} custom-call(bf16[2,128,1536]{2,1,0:T(8,128)(2,1)} %bitcast.52), custom_call_target="tpu_custom_call" | custom-call | tf_op jit(solution)/shard_map/gather_rows/pallas_call | solution.py:283
  384.1 0.0 copy-done.3
  384.1 0.0 copy-start.1
  384.2 2.9 copy-done.1
  387.1 23.5 %schur_rows.1 = f32[256,6656]{1,0:T(8,128)} custom-call(s32[1]{0:T(128)} %bitcast.7.me_ref, f32[256,6656]{1,0:T(8,128)S(1)} %copy-done.1, bf16[256,1536]{1,0:T(8,128)(2,1)S(1)} %copy-done.3, bf16[8192,1536]{1,0:T(8,128)(2,1)} %bitcast.53), custom_call_target="tpu_custom_call" | custom-call | tf_op jit(solution)/shard_map/schur_rows/pallas_call | solution.py:625
  (6 shorter events, 0.1 us)
Async XLA Ops:
  1.7 2.2 copy-start.2
  16.5 3.2 copy-start
  19.7 12.0 %copy-start.6 = (s32[1,128]{1,0:T(1,128)S(1)}, s32[1,128]{1,0:T(1,128)}, u32[]{:S(2)}) copy-start(s32[1,128]{1,0:T(1,128)} %param.9) | copy-start | bytes 1540
  19.7 12.0 %copy-start.7 = (s32[1,128]{1,0:T(1,128)S(1)}, s32[1,128]{1,0:T(1,128)}, u32[]{:S(2)}) copy-start(s32[1,128]{1,0:T(1,128)} %param.8) | copy-start | bytes 1540
  19.7 12.0 %copy-start.8 = (s32[1,128,1]{1,2,0:T(1,128)S(1)}, s32[1,128,1]{1,2,0:T(1,128)}, u32[]{:S(2)}) copy-start(s32[1,128,1]{1,2,0:T(1,128)} %param.7) | copy-start | bytes 1540
  19.7 259.1 %all-to-all-start = ((bf16[128,2,128,128]{3,2,1,0:T(8,128)(2,1)}), bf16[128,2,128,128]{3,2,1,0:T(8,128)(2,1)}, u32[]{:S(2)}, u32[]{:S(2)}) async-start(bf16[128,2,128,128]{3,2,1,0:T(8,128)(2,1)} %bitcast.50), calls=%async_computation | async-start | bytes 16777216 | tf_op jit(solution)/shard_map/all_to_all | solution.py:682
  276.5 1.2 copy-start.4
  277.7 1.1 copy-start.5
  292.8 91.3 %copy-start.3 = (bf16[256,1536]{1,0:T(8,128)(2,1)S(1)}, bf16[256,1536]{1,0:T(8,128)(2,1)}, u32[]{:S(2)}) copy-start(bf16[256,1536]{1,0:T(8,128)(2,1)} %get-tuple-element.13.rows_ref) | copy-start | bytes 2359300
  384.1 2.9 copy-start.1

commit v3 on v2

--- a/solution.py
+++ b/solution.py
@@ -12,6 +12,8 @@
 TB = 128
 SUB = 16
 SLOTS = 2
+GROUPS = 4
+LABEL_ROWS = 16
 MIB = 1 << 20
 
 
@@ -165,7 +167,8 @@
             pl.semaphore_signal(barrier, inc=1, device_id={"front": peer}, device_id_type=MESH)
         return barrier
 
-    def gather(self, own, out, ring_recv, side_recv, own_recv, local_sem, send_sem):
+    def gather(self, own, out, sems, after=None):
+        ring_recv, side_recv, own_recv, local_sem, send_sem = sems
         core = self.core
 
         def piece(da, db, s, other=False):
@@ -249,17 +252,37 @@
             (2, 2, 0, []),
             (2, 2, 1, []),
         ]
-        for da, db, s, onward in steps:
+        def take_own():
+            arrive(piece(0, 0, 1 - core, True), own_recv.at[1], here)
+            when(here, rest.wait)
+
+        def take_side(da, db):
+            parts = [s for at_a, at_b, s, _ in steps if (at_a, at_b) == (da, db)]
+            for s in parts:
+                arrive(
+                    piece(da, db, s, True), side_recv.at[da, db, s or 0], self.live(da, db, True)
+                )
+
+        for number, (da, db, s, onward) in enumerate(steps):
             arrive(piece(da, db, s), ring_recv.at[da, db, s or 0], self.live(da, db))
             for part, to in onward:
                 give(da, db, part, to)
             give(da, db, s, "s")
-        arrive(piece(0, 0, 1 - core, True), own_recv.at[1], here)
-        when(here, rest.wait)
-        for da, db, s, _ in steps:
-            arrive(piece(da, db, s, True), side_recv.at[da, db, s or 0], self.live(da, db, True))
+            if after is not None:
+                after(number, take_own, take_side)
+        if after is None:
+            take_own()
+            for da, db in UNITS[1:]:
+                take_side(da, db)
         for condition, wait in self.late:
             when(condition, wait)
+
+
+UNITS = [
+    (0, 0), (0, 3), (0, 1), (3, 0), (1, 0), (0, 2), (3, 3), (1, 3),
+    (3, 1), (1, 1), (2, 0), (3, 2), (1, 2), (2, 3), (2, 1), (2, 2),
+]
+BATCHES = {5: (0, 6, 0, 5), 9: (6, 10, 5, 8), 11: (10, 11, 8, 10), 15: (11, 13, 10, 11), 21: (13, 16, 11, 16)}
 
 
 RING_SEMS = [
@@ -271,25 +294,78 @@
 ]
 
 
-def gather_kernel(rows_ref, out_ref, *sems):
+def schur_kernel(rows_ref, rest_ref, out_ref, gathered, rest_sem, *sems):
     ring = Ring(PANELS)
     pl.semaphore_wait(ring.greet(), len(ring.peer))
-    ring.gather(lambda h: rows_ref.at[h], out_ref, *sems)
-
-
-def gather_rows(rows):
+    below = ring.me >= PANELS
+    fill = pltpu.make_async_copy(rest_ref, out_ref, rest_sem)
+
+    @pl.when(below)
+    def _():
+        fill.start()
+
+    @pl.when(jnp.logical_not(below))
+    def _():
+        out_ref[...] = jnp.zeros_like(out_ref)
+
+    def after(step, take_own, take_side):
+        if step not in BATCHES:
+            return
+        own_from, own_to, side_from, side_to = BATCHES[step]
+        if own_from == 0:
+            take_own()
+
+            @pl.when(below)
+            def _():
+                fill.wait()
+
+        for da, db in UNITS[max(side_from, 1) : side_to]:
+            take_side(da, db)
+
+        def use(n, c):
+            side = n >= own_to - own_from
+            at = jnp.where(side, n - (own_to - own_from) + side_from, n + own_from)
+            da = sum(jnp.where(at == i, unit[0], 0) for i, unit in enumerate(UNITS))
+            db = sum(jnp.where(at == i, unit[1], 0) for i, unit in enumerate(UNITS))
+            chip = jnp.where(side, ring.chip(da, db, True), ring.chip(da, db))
+            half = jnp.where(side, 1 - ring.core, ring.core)
+
+            @pl.when(below & (chip * 2 >= PANELS))
+            def _():
+                unit = gathered[pl.ds(chip * 2, 2), half].reshape(PW, rows_ref.shape[1])
+                term = dot_nt(rows_ref[...], unit)
+                for core in range(2):
+                    start = (chip * 2 + core - PANELS) * PW + half * TB
+                    at_columns = pl.ds(pl.multiple_of(start, TB), TB)
+                    out_ref[:, at_columns] -= term[:, core * TB : (core + 1) * TB]
+
+            return c
+
+        lax.fori_loop(0, own_to - own_from + side_to - side_from, use, 0)
+
+    ring.gather(lambda h: rows_ref.at[pl.ds(h * TB, TB)], gathered, sems, after)
+
+
+def gather_schur(rows, rest):
     fronts = lax.axis_size("front")
-    halved = rows.reshape(2, rows.shape[0] // 2, rows.shape[1])
-    out = pl.pallas_call(
-        gather_kernel,
-        in_specs=[pl.BlockSpec(memory_space=pl.ANY)],
-        out_specs=pl.BlockSpec(memory_space=pl.ANY),
-        out_shape=jax.ShapeDtypeStruct((fronts,) + halved.shape, rows.dtype),
-        scratch_shapes=RING_SEMS,
-        compiler_params=pltpu.CompilerParams(collective_id=1, has_side_effects=True),
-        name="gather_rows",
-    )(halved)
-    return out.reshape(fronts * rows.shape[0], rows.shape[1])
+    return pl.pallas_call(
+        schur_kernel,
+        in_specs=[
+            pl.BlockSpec(memory_space=pltpu.VMEM),
+            pl.BlockSpec(memory_space=pl.ANY),
+        ],
+        out_specs=pl.BlockSpec(memory_space=pltpu.VMEM),
+        out_shape=jax.ShapeDtypeStruct(rest.shape, jnp.float32),
+        scratch_shapes=[
+            pltpu.VMEM((fronts, 2, TB, rows.shape[1]), jnp.bfloat16),
+            pltpu.SemaphoreType.DMA,
+        ]
+        + RING_SEMS,
+        compiler_params=pltpu.CompilerParams(
+            collective_id=1, has_side_effects=True, vmem_limit_bytes=60 * MIB
+        ),
+        name="gather_schur",
+    )(rows, rest)
 
 
 def spread_kernel(front_ref, out_ref, share, deal_recv, deal_send, *sems):
@@ -364,7 +440,7 @@
         def _():
             far(0, piece).wait_recv()
 
-    ring.gather(lambda h: share.at[h], out_ref, *sems)
+    ring.gather(lambda h: share.at[h], out_ref, sems)
     for i in range(PANELS):
         mine = [piece for piece in pieces if piece[0] == i]
 
@@ -395,7 +471,9 @@
             pltpu.SemaphoreType.DMA((2, fronts)),
         ]
         + RING_SEMS,
-        compiler_params=pltpu.CompilerParams(collective_id=2, has_side_effects=True),
+        compiler_params=pltpu.CompilerParams(
+            collective_id=2, has_side_effects=True, vmem_limit_bytes=60 * MIB
+        ),
         name="spread_pivots",
     )(front)
 
@@ -488,7 +566,7 @@
             jax.ShapeDtypeStruct((PANELS, PW, PW), jnp.float32),
             jax.ShapeDtypeStruct((PW, order), jnp.float32),
         ],
-        compiler_params=pltpu.CompilerParams(vmem_limit_bytes=48 * MIB),
+        compiler_params=pltpu.CompilerParams(vmem_limit_bytes=60 * MIB),
         cost_estimate=pl.CostEstimate(
             flops=80_000_000_000, bytes_accessed=20_000_000, transcendentals=0
         ),
@@ -496,35 +574,50 @@
     )(me, shares)
 
 
-def pack_kernel(pick_ref, tiles_ref, outbox_ref, sem):
-    count = outbox_ref.shape[0]
+def pack_kernel(pick_ref, tiles_ref, labels_ref, outbox_ref, sem, label_sem):
+    tail = outbox_ref.shape[0] // GROUPS - PANELS
+    labels = pltpu.make_async_copy(
+        labels_ref, outbox_ref.at[:, pl.ds(SLOTS * TB, LABEL_ROWS)], label_sem
+    )
+    labels.start()
 
     def send(i, c):
-        pltpu.make_async_copy(tiles_ref.at[pick_ref[i]], outbox_ref.at[i], sem).start()
+        device = i // tail * (tail + PANELS) + PANELS + i % tail
+        for s in range(SLOTS):
+            pltpu.make_async_copy(
+                tiles_ref.at[pick_ref[device * SLOTS + s]],
+                outbox_ref.at[device, pl.ds(s * TB, TB)],
+                sem,
+            ).start()
         return c
 
-    lax.fori_loop(0, count, send, 0, unroll=8)
-    pltpu.make_async_copy(outbox_ref, outbox_ref, sem).wait()
-
-
-def pack_tiles(pick, tiles):
-    count = pick.shape[0]
+    lax.fori_loop(0, GROUPS * tail, send, 0, unroll=4)
+    filled = outbox_ref.at[pl.ds(0, GROUPS * tail), pl.ds(0, SLOTS * TB)]
+    pltpu.make_async_copy(filled, filled, sem).wait()
+    labels.wait()
+
+
+def pack_tiles(pick, tiles, labels):
+    devices = labels.shape[0]
     return pl.pallas_call(
         pack_kernel,
         grid_spec=pltpu.PrefetchScalarGridSpec(
             num_scalar_prefetch=1,
             grid=(1,),
-            in_specs=[pl.BlockSpec(tiles.shape, lambda i, p: (0, 0, 0))],
+            in_specs=[
+                pl.BlockSpec(tiles.shape, lambda i, p: (0, 0, 0)),
+                pl.BlockSpec(labels.shape, lambda i, p: (0, 0, 0)),
+            ],
             out_specs=pl.BlockSpec(memory_space=pl.ANY),
-            scratch_shapes=[pltpu.SemaphoreType.DMA],
+            scratch_shapes=[pltpu.SemaphoreType.DMA, pltpu.SemaphoreType.DMA],
         ),
-        out_shape=jax.ShapeDtypeStruct((count, TB, TB), jnp.bfloat16),
-        compiler_params=pltpu.CompilerParams(vmem_limit_bytes=32 * MIB),
+        out_shape=jax.ShapeDtypeStruct((devices, SLOTS * TB + LABEL_ROWS, TB), jnp.bfloat16),
+        compiler_params=pltpu.CompilerParams(vmem_limit_bytes=60 * MIB),
         name="pack_tiles",
-    )(pick, tiles)
-
-
-CHUNK = 32
+    )(pick, tiles, labels)
+
+
+CHUNK = 16
 
 
 def solve_kernel(
@@ -539,7 +632,9 @@
 
     def fetch(c):
         part = pl.ds(c * CHUNK, CHUNK)
-        return pltpu.make_async_copy(inbox_ref.at[part], landed.at[part], sems.at[c])
+        return pltpu.make_async_copy(
+            inbox_ref.at[part, pl.ds(0, SLOTS * TB)], landed.at[part], sems.at[c]
+        )
 
     for c in range(chunks):
         fetch(c).start()
@@ -549,15 +644,16 @@
         fetch(c).wait()
 
         def add(i, carry):
-            code = tags_ref[i]
-
-            @pl.when(code >= 0)
-            def _():
-                place = (
-                    pl.ds(pl.multiple_of((code // 64) * TB, TB), TB),
-                    pl.ds(pl.multiple_of((code % 64) * TB, TB), TB),
-                )
-                work[place] += landed[i].astype(jnp.float32)
+            for s in range(SLOTS):
+                code = tags_ref[i * SLOTS + s]
+
+                @pl.when(code >= 0)
+                def _():
+                    place = (
+                        pl.ds(pl.multiple_of((code // 64) * TB, TB), TB),
+                        pl.ds(pl.multiple_of((code % 64) * TB, TB), TB),
+                    )
+                    work[place] += landed[i, s * TB : (s + 1) * TB].astype(jnp.float32)
 
             return carry
 
@@ -600,7 +696,7 @@
             ],
             scratch_shapes=[
                 pltpu.VMEM((PW, order), jnp.float32),
-                pltpu.VMEM(inbox.shape, jnp.bfloat16),
+                pltpu.VMEM((count, SLOTS * TB, TB), jnp.bfloat16),
                 pltpu.SemaphoreType.DMA((count // CHUNK + 1,)),
                 pltpu.SemaphoreType.DMA,
             ],
@@ -610,34 +706,9 @@
             jax.ShapeDtypeStruct((PW, pivots), jnp.bfloat16),
             jax.ShapeDtypeStruct((PW, order - pivots), jnp.float32),
         ],
-        compiler_params=pltpu.CompilerParams(vmem_limit_bytes=56 * MIB),
+        compiler_params=pltpu.CompilerParams(vmem_limit_bytes=60 * MIB),
         name="solve_rows",
     )(tags, me, front, inbox, bits, inverse, own)
-
-
-def schur_kernel(me_ref, rest_ref, rows_ref, others_ref, out_ref):
-    term = dot_nt(rows_ref[...], others_ref[...])
-    out_ref[...] = jnp.where(me_ref[0] >= PANELS, rest_ref[...] - term, 0.0)
-
-
-def schur_rows(me, rest, rows, gathered):
-    width = rest.shape[1]
-    return pl.pallas_call(
-        schur_kernel,
-        grid_spec=pltpu.PrefetchScalarGridSpec(
-            num_scalar_prefetch=1,
-            grid=(width // PW,),
-            in_specs=[
-                pl.BlockSpec((PW, PW), lambda j, m: (0, j)),
-                pl.BlockSpec(rows.shape, lambda j, m: (0, 0)),
-                pl.BlockSpec((PW, rows.shape[1]), lambda j, m: (j + PANELS, 0)),
-            ],
-            out_specs=pl.BlockSpec((PW, PW), lambda j, m: (0, j)),
-        ),
-        out_shape=jax.ShapeDtypeStruct(rest.shape, jnp.float32),
-        compiler_params=pltpu.CompilerParams(vmem_limit_bytes=32 * MIB),
-        name="schur_rows",
-    )(me, rest, rows, gathered)
 
 
 def on_device(front_matrix, child_tiles, tile_route, tile_row, tile_col):
@@ -649,45 +720,34 @@
     devices = groups * fronts
     tail = fronts - PANELS
     me = lax.axis_index("front")
-    mine = lax.axis_index("group") * fronts + me
     shares = spread_pivots(work)
 
     target = tile_route[0, :, 0]
     destination = target // tail * fronts + PANELS + target % tail
-    code = (destination * 2 + tile_row[0]) * 64 + tile_col[0]
+    label = tile_row[0] * 64 + tile_col[0]
     positions = jnp.arange(count, dtype=jnp.int32)
     meets = destination[None, :] == jnp.arange(devices, dtype=jnp.int32)[:, None]
     first = jnp.min(jnp.where(meets, positions[None, :], count), axis=1)
     last = jnp.max(jnp.where(meets, positions[None, :], -1), axis=1)
     pick = jnp.stack([jnp.where(first < count, first, 0), jnp.maximum(last, 0)], axis=1)
-    codes = lax.all_gather(code, ("group", "front"), axis=0).reshape(devices, count)
-    here = codes // 128 == mine
-    from_first = jnp.min(jnp.where(here, positions[None, :], count), axis=1)
-    from_last = jnp.max(jnp.where(here, positions[None, :], -1), axis=1)
-    label = codes % 128
-    tag_first = jnp.max(
-        jnp.where(positions[None, :] == from_first[:, None], label, -1), axis=1
+    here = positions[None, :] == first[:, None]
+    label_first = jnp.max(jnp.where(here, label[None, :], -1), axis=1)
+    here = (positions[None, :] == last[:, None]) & (last != first)[:, None]
+    label_last = jnp.max(jnp.where(here, label[None, :], -1), axis=1)
+    lane = jnp.arange(TB, dtype=jnp.int32)[None, :]
+    labels = jnp.where(lane == 0, label_first[:, None], label_last[:, None])
+    labels = jnp.broadcast_to(
+        labels.astype(jnp.bfloat16)[:, None, :], (devices, LABEL_ROWS, TB)
     )
-    tag_last = jnp.max(
-        jnp.where(
-            (positions[None, :] == from_last[:, None]) & (from_last != from_first)[:, None],
-            label,
-            -1,
-        ),
-        axis=1,
-    )
-    tags = jnp.stack([tag_first, tag_last], axis=1).reshape(devices * SLOTS)
-
-    outbox = pack_tiles(pick.reshape(devices * SLOTS), tiles)
-    inbox = lax.all_to_all(
-        outbox.reshape(devices, SLOTS, TB, TB), ("group", "front"), 0, 0, tiled=True
-    ).reshape(devices * SLOTS, TB, TB)
+    outbox = pack_tiles(pick.reshape(devices * SLOTS), tiles, labels)
+    outbox, shares = lax.optimization_barrier((outbox, shares))
+    inbox = lax.all_to_all(outbox, ("group", "front"), 0, 0, tiled=True)
+    tags = inbox[:, SLOTS * TB, :SLOTS].astype(jnp.int32).reshape(devices * SLOTS)
 
     self = me.astype(jnp.int32).reshape(1)
     bits, inverse, own = factor_pivots(self, shares)
     factor, rows, rest = solve_rows(tags, self, work, inbox, bits, inverse, own)
-    gathered = gather_rows(rows)
-    schur = schur_rows(self, rest, rows, gathered)
+    schur = gather_schur(rows, rest)
     return (factor[None], schur[None])
 
 

time: 411 us -> 282 us (0.69)
  blocking collectives: 127 us -> 0 us
  waiting for transfers between devices: 0.01 us -> 33.6 us
  Pallas kernels: 258 us -> 229 us
  starting transfers between devices: 12 us -> 7.33 us
    all_gather x1 -> x0, blocking collectives: 127 us -> none  [on_device(): lax.all_gather(code, ('group', 'front'), axis=0).reshape(devices, count)]
    all_to_all x1, waiting for transfers between devices: 0.01 us -> 33.6 us  [on_device(): inbox = lax.all_to_all(outbox, ('group', 'front'), 0, 0, tiled=True)]
    pallas_call x2 -> x1, Pallas kernels: 115 us -> 87.1 us  [gather_schur(): pl.pallas_call(schur_kernel, in_specs=[pl.BlockSpec(memory_space=pltpu.VM...]
    pallas_call x1, Pallas kernels: 12.5 us -> 6.07 us  [pack_tiles(): pl.pallas_call(pack_kernel, grid_spec=pltpu.PrefetchScalarGridSpec(num_sc...]
    all_to_all x1, starting transfers between devices: 12 us -> 7.33 us  [on_device(): inbox = lax.all_to_all(outbox, ('group', 'front'), 0, 0, tiled=True)]
    unnamed x18 -> x5, local copies, waits for them, and re-layouts: 10.6 us -> 6.28 us
  transfers between devices with their start and end apart: 1 -> 1, of which waited for: 0 -> 1; matrix products, arithmetic and copies ran while one was open for 0% -> 0% of each run, Pallas kernels for 28% -> 25%
where the time goes in v3:
time: 282 us
  Pallas kernels  229 us (81%)
  waiting for transfers between devices  33.6 us (12%)
  local copies, waits for them, and re-layouts  8.69 us (3%)
  starting transfers between devices  7.33 us (3%)
    pallas_call x1, Pallas kernels, gather_schur(): pl.pallas_call(schur_kernel, in_specs=[pl.BlockSpec(memory_space=pltpu.VM...  87.1 us
    pallas_call x1, Pallas kernels, factor_pivots(): pl.pallas_call(pivot_kernel, grid_spec=pltpu.PrefetchScalarGridSpec(num_s...  71.1 us
    pallas_call x1, Pallas kernels, spread_pivots(): pl.pallas_call(spread_kernel, in_specs=[pl.BlockSpec(memory_space=pl.ANY)...  50.6 us
    all_to_all x1, waiting for transfers between devices, on_device(): inbox = lax.all_to_all(outbox, ('group', 'front'), 0, 0, tiled=True)  33.6 us
    pallas_call x1, Pallas kernels, solve_rows(): pl.pallas_call(solve_kernel, grid_spec=pltpu.PrefetchScalarGridSpec(num_s...  14.1 us
    all_to_all x1, starting transfers between devices, on_device(): inbox = lax.all_to_all(outbox, ('group', 'front'), 0, 0, tiled=True)  7.33 us
    unnamed x5, local copies, waits for them, and re-layouts  6.28 us
    pallas_call x1, Pallas kernels, pack_tiles(): pl.pallas_call(pack_kernel, grid_spec=pltpu.PrefetchScalarGridSpec(num_sc...  6.07 us
  transfers between devices with their start and end apart: 1, of which 1 were waited for; matrix products, arithmetic and copies ran while one was open for 0% of the time, Pallas kernels for 25%

profile of v3, /device:TPU:1, one launch (start us, length us, event | category | flops | bytes accessed | tf_op | source)
XLA Modules:
  0.0 281.6 jit_solution(2160532262626007477)
XLA Ops:
  0.6 0.7 fusion.3
  1.3 0.1 select_reduce_fusion.3
  1.5 0.1 copy.8
  1.6 0.7 reshape.112.pick_ref
  2.3 0.0 copy-start
  2.3 0.0 copy-start.1
  2.3 50.6 %spread_pivots.1.shares_ref = f32[32,2,24,896]{3,2,1,0:T(8,128)} custom-call(f32[256,8192]{1,0:T(8,128)} %bitcast.26), custom_call_target="tpu_custom_call" | custom-call | tf_op jit(solution)/shard_map/spread_pivots/pallas_call | solution.py:463
  52.9 0.0 copy-done
  52.9 0.0 copy-done.1
  52.9 0.2 select_reduce_fusion.1
  53.1 0.1 select_convert_fusion
  53.2 0.9 broadcast_in_dim.99.labels_ref
  54.1 6.1 %pack_tiles.1 = bf16[128,272,128]{2,1,0:T(8,128)(2,1)} custom-call(s32[256]{0:T(256)} %reshape.112.pick_ref, bf16[128,128,128]{2,1,0:T(8,128)(2,1)} %bitcast.29, bf16[128,16,128]{2,1,0:T(8,128)(2,1)} %broadcast_in_dim.99.labels_ref), custom_call_target="tpu_custom_call" | custom-call | tf_op jit(solution)/shard_map/pack_tiles/pallas_call | solution.py:602
  60.2 7.3 %all-to-all-start = ((bf16[128,272,128]{2,1,0:T(8,128)(2,1)}), bf16[128,272,128]{2,1,0:T(8,128)(2,1)}, u32[]{:S(2)}, u32[]{:S(2)}) async-start(bf16[128,272,128]{2,1,0:T(8,128)(2,1)} %pack_tiles.1), calls=%async_computation | async-start | bytes 17825792 | tf_op jit(solution)/shard_map/all_to_all | solution.py:744
  67.5 71.1 %factor_pivots.1 = (bf16[1536,1536]{1,0:T(8,128)(2,1)}, f32[6,256,256]{2,1,0:T(8,128)}, f32[256,1536]{1,0:T(8,128)}) custom-call(s32[1]{0:T(128)} %bitcast.8.me_ref, f32[32,2,24,896]{3,2,1,0:T(8,128)} %spread_pivots.1.shares_ref), custom_call_target="tpu_custom_call" | custom-call | flops 80000000000 | bytes 20000000 | tf_op jit(solution)/shard_map/factor_pivots/pallas_call | solution.py:548
  138.7 33.6 %all-to-all-done.inbox_ref = bf16[128,272,128]{2,1,0:T(8,128)(2,1)} async-done(((bf16[128,272,128]{2,1,0:T(8,128)(2,1)}), bf16[128,272,128]{2,1,0:T(8,128)(2,1)}, u32[]{:S(2)}, u32[]{:S(2)}) %all-to-all-start) | async-done | bytes 8912928 | tf_op jit(solution)/shard_map/all_to_all | solution.py:744
  172.2 1.2 fusion
  173.4 0.7 reshape.114.tags_ref
  174.1 14.1 %solve_rows.1 = (f32[256,1536]{1,0:T(8,128)}, bf16[256,1536]{1,0:T(8,128)(2,1)}, f32[256,6656]{1,0:T(8,128)}) custom-call(s32[256]{0:T(256)} %reshape.114.tags_ref, s32[1]{0:T(128)} %bitcast.8.me_ref, f32[256,8192]{1,0:T(8,128)} %bitcast.27, bf16[128,272,128]{2,1,0:T(8,128)(2,1)} %all-to-all-done.inbox_ref, bf16[1536,1536]{1,0:T(8,128)(2,1)} %get-tuple-element.12.bits_ref, ...), custom_call_target="tpu_custom_call" | custom-call | tf_op jit(solution)/shard_map/solve_rows/pallas_call | solution.py:680
  188.2 87.1 %gather_schur.1 = f32[256,6656]{1,0:T(8,128)} custom-call(bf16[256,1536]{1,0:T(8,128)(2,1)} %get-tuple-element.16.rows_ref, f32[256,6656]{1,0:T(8,128)} %get-tuple-element.17.rest_ref), custom_call_target="tpu_custom_call" | custom-call | tf_op jit(solution)/shard_map/gather_schur/pallas_call | solution.py:351
  275.3 6.3 %copy.10 = f32[1,256,6656]{2,1,0:T(8,128)} copy(f32[1,256,6656]{2,1,0:T(8,128)} %bitcast.28) | data formatting | bytes 13631488
  (6 shorter events, 0.0 us)
Async XLA Ops:
  2.3 50.6 %copy-start = (s32[1,128]{1,0:T(1,128)S(1)}, s32[1,128]{1,0:T(1,128)}, u32[]{:S(2)}) copy-start(s32[1,128]{1,0:T(1,128)} %param.9) | copy-start | bytes 1540
  2.3 50.6 %copy-start.1 = (s32[1,128]{1,0:T(1,128)S(1)}, s32[1,128]{1,0:T(1,128)}, u32[]{:S(2)}) copy-start(s32[1,128]{1,0:T(1,128)} %param.8) | copy-start | bytes 1540
  60.2 112.0 %all-to-all-start = ((bf16[128,272,128]{2,1,0:T(8,128)(2,1)}), bf16[128,272,128]{2,1,0:T(8,128)(2,1)}, u32[]{:S(2)}, u32[]{:S(2)}) async-start(bf16[128,272,128]{2,1,0:T(8,128)(2,1)} %pack_tiles.1), calls=%async_computation | async-start | bytes 17825792 | tf_op jit(solution)/shard_map/all_to_all | solution.py:744

commit v4 on v3

--- a/solution.py
+++ b/solution.py
@@ -12,8 +12,11 @@
 TB = 128
 SUB = 16
 SLOTS = 2
-GROUPS = 4
 LABEL_ROWS = 16
+AHEAD = 4
+EARLY = 10
+EACH = 1
+STEPS = 22
 MIB = 1 << 20
 
 
@@ -167,7 +170,7 @@
             pl.semaphore_signal(barrier, inc=1, device_id={"front": peer}, device_id_type=MESH)
         return barrier
 
-    def gather(self, own, out, sems, after=None):
+    def gather(self, own, out, sems, after=None, taken=False):
         ring_recv, side_recv, own_recv, local_sem, send_sem = sems
         core = self.core
 
@@ -270,7 +273,7 @@
             give(da, db, s, "s")
             if after is not None:
                 after(number, take_own, take_side)
-        if after is None:
+        if not taken:
             take_own()
             for da, db in UNITS[1:]:
                 take_side(da, db)
@@ -343,7 +346,7 @@
 
         lax.fori_loop(0, own_to - own_from + side_to - side_from, use, 0)
 
-    ring.gather(lambda h: rows_ref.at[pl.ds(h * TB, TB)], gathered, sems, after)
+    ring.gather(lambda h: rows_ref.at[pl.ds(h * TB, TB)], gathered, sems, after, taken=True)
 
 
 def gather_schur(rows, rest):
@@ -368,25 +371,8 @@
     )(rows, rest)
 
 
-def spread_kernel(front_ref, out_ref, share, deal_recv, deal_send, *sems):
-    fronts = out_ref.shape[0]
-    ring = Ring(0)
+def deal_shares(ring, front_ref, share, deal_recv, deal_send, fronts):
     me = ring.me
-    barrier = ring.greet()
-    for i in range(PANELS):
-
-        @pl.when(me != i)
-        def _():
-            pl.semaphore_signal(barrier, inc=1, device_id={"front": i}, device_id_type=MESH)
-
-    @pl.when(me < PANELS)
-    def _():
-        pl.semaphore_wait(barrier, len(ring.peer) + fronts - 1)
-
-    @pl.when(me >= PANELS)
-    def _():
-        pl.semaphore_wait(barrier, len(ring.peer))
-
     pieces = []
     for i in range(PANELS):
         for segment in share_segments(i):
@@ -413,82 +399,151 @@
     def near(piece):
         return pltpu.make_async_copy(source(me, piece), target(piece), deal_recv.at[piece[1]])
 
+    def each(i, action):
+        mine = [piece for piece in pieces if piece[0] == i]
+
+        def one(f, c):
+            @pl.when(f != me)
+            def _():
+                for piece in mine:
+                    action(far(f, piece))
+
+            return c
+
+        lax.fori_loop(0, fronts, one, 0)
+        return mine
+
     for i in range(PANELS):
-        mine = [piece for piece in pieces if piece[0] == i]
 
         @pl.when(me == i)
         def _():
-            def deal(f, c):
-                @pl.when(f != me)
-                def _():
-                    for piece in mine:
-                        far(f, piece).start()
-
-                return c
-
-            lax.fori_loop(0, fronts, deal, 0)
-            for piece in mine:
+            for piece in each(i, lambda copy: copy.start()):
                 near(piece).start()
 
-    for piece in pieces:
-
-        @pl.when(me == piece[0])
-        def _():
-            near(piece).wait()
-
-        @pl.when(me != piece[0])
-        def _():
-            far(0, piece).wait_recv()
-
-    ring.gather(lambda h: share.at[h], out_ref, sems)
-    for i in range(PANELS):
-        mine = [piece for piece in pieces if piece[0] == i]
-
-        @pl.when(me == i)
-        def _():
-            def done(f, c):
-                @pl.when(f != me)
-                def _():
-                    for piece in mine:
-                        far(f, piece).wait_send()
-
-                return c
-
-            lax.fori_loop(0, fronts, done, 0)
-
-
-def spread_pivots(front):
-    fronts = lax.axis_size("front")
-    share = (2, PANELS // 2 * (PW // fronts), (PANELS + 1) * PW // 2)
-    return pl.pallas_call(
-        spread_kernel,
-        in_specs=[pl.BlockSpec(memory_space=pl.ANY)],
-        out_specs=pl.BlockSpec(memory_space=pl.ANY),
-        out_shape=jax.ShapeDtypeStruct((fronts,) + share, jnp.float32),
-        scratch_shapes=[
-            pltpu.VMEM(share, jnp.float32),
-            pltpu.SemaphoreType.DMA((9,)),
-            pltpu.SemaphoreType.DMA((2, fronts)),
-        ]
-        + RING_SEMS,
-        compiler_params=pltpu.CompilerParams(
-            collective_id=2, has_side_effects=True, vmem_limit_bytes=60 * MIB
-        ),
-        name="spread_pivots",
-    )(front)
-
-
-def pivot_kernel(me_ref, shares_ref, bits_ref, inverse_ref, own_ref, work, sem):
-    high = lax.Precision.HIGHEST
-    fronts = shares_ref.shape[0]
+    def wait_share():
+        for piece in pieces:
+
+            @pl.when(me == piece[0])
+            def _():
+                near(piece).wait()
+
+            @pl.when(me != piece[0])
+            def _():
+                far(0, piece).wait_recv()
+
+    def wait_sent():
+        for i in range(PANELS):
+
+            @pl.when(me == i)
+            def _():
+                each(i, lambda copy: copy.wait_send())
+
+    return wait_share, wait_sent
+
+
+def exchange_kernel(
+    pick_ref, front_ref, tiles_ref, labels_ref,
+    bits_ref, inverse_ref, own_ref, inbox_ref,
+    work, tiles, outbox, share, shares,
+    tile_sem, unpack_sem, ship_send, ship_recv, deal_recv, deal_send, *sems,
+):
+    devices = inbox_ref.shape[0]
+    fronts = shares.shape[0]
+    tail = fronts - PANELS
+    ring = Ring(0)
+    me = ring.me
+    mine = lax.axis_index("group") * fronts + me
+    fetch = pltpu.make_async_copy(tiles_ref, tiles, tile_sem)
+    fetch.start()
+
+    def where_is(device):
+        return {"group": device // fronts, "front": device % fronts}
+
+    barrier = pltpu.get_barrier_semaphore()
+
+    def greet(k, c):
+        other = where_is((mine + k) % devices)
+        pl.semaphore_signal(barrier, inc=1, device_id=other, device_id_type=MESH)
+        return c
+
+    lax.fori_loop(1, devices, greet, 0)
+    pl.semaphore_wait(barrier, devices - 1)
+    wait_share, wait_sent = deal_shares(ring, front_ref, share, deal_recv, deal_send, fronts)
+
+    fetch.wait()
+
+    def pack(i, c):
+        device = i // tail * fronts + PANELS + i % tail
+        for s in range(SLOTS):
+            outbox[device, s * TB : (s + 1) * TB] = tiles[pick_ref[device * SLOTS + s]]
+        outbox[device, SLOTS * TB :] = labels_ref[device]
+        return c
+
+    lax.fori_loop(0, devices // fronts * tail, pack, 0)
+    def ship(k):
+        device = (mine + k * 37) % devices
+        return device, pltpu.make_async_remote_copy(
+            src_ref=outbox.at[device],
+            dst_ref=inbox_ref.at[mine],
+            send_sem=ship_send.at[k],
+            recv_sem=ship_recv.at[k],
+            device_id=where_is(device),
+            device_id_type=MESH,
+        )
+
+    def start(k, c):
+        device, copy = ship(k)
+        pl.when(device % fronts >= PANELS)(copy.start)
+        return c
+
+    def left(k, c):
+        device, copy = ship(k)
+        pl.when(device % fronts >= PANELS)(copy.wait_send)
+        return c
+
+    def pace(k, c):
+        start(k, c)
+        return left(k - AHEAD, c)
+
+    lax.fori_loop(1, 1 + AHEAD, start, 0)
+    begun = 1 + AHEAD + EARLY
+    lax.fori_loop(1 + AHEAD, begun, pace, 0)
+
+    def after(step, take_own, take_side):
+        lax.fori_loop(begun + step * EACH, begun + (step + 1) * EACH, pace, 0)
+
+    wait_share()
+    ring.gather(lambda h: share.at[h], shares, sems, after)
+    begun = begun + STEPS * EACH
+
+    lax.fori_loop(begun, devices, start, 0)
+    keep = pltpu.make_async_copy(outbox.at[mine], inbox_ref.at[mine], ship_recv.at[0])
+    below = me >= PANELS
+    pl.when(below)(keep.start)
+
     for i in range(PANELS):
         for half, group, source, target, width in share_segments(i):
             pltpu.make_async_copy(
-                shares_ref.at[:, half, pl.ds(group * 8, 8), pl.ds(source, width)],
+                shares.at[:, half, pl.ds(group * 8, 8), pl.ds(source, width)],
                 work.at[pl.ds(i * fronts, fronts), :, pl.ds(target, width)],
-                sem,
+                unpack_sem,
             ).start()
-    pltpu.make_async_copy(shares_ref, shares_ref, sem).wait()
+    pltpu.make_async_copy(shares, shares, unpack_sem).wait()
+    factor_pivots(me, work, bits_ref, inverse_ref, own_ref)
+
+    pl.when(below)(keep.wait)
+
+    def landed(k, c):
+        pl.when(below)(ship(k)[1].wait_recv)
+        return c
+
+    lax.fori_loop(begun - AHEAD, devices, left, 0)
+    lax.fori_loop(1, devices, landed, 0)
+    wait_sent()
+
+
+def factor_pivots(me, work, bits_ref, inverse_ref, own_ref):
+    high = lax.Precision.HIGHEST
 
     def cols(i):
         return pl.ds(pl.multiple_of(i * PW, PW), PW)
@@ -534,7 +589,7 @@
         return carry
 
     lax.fori_loop(0, PANELS, panel, 0)
-    me = jnp.minimum(me_ref[0], PANELS - 1)
+    me = jnp.minimum(me, PANELS - 1)
 
     def out(j, c):
         own_ref[:, cols(j)] = jnp.where(j <= me, load(me, j), 0.0)
@@ -543,78 +598,47 @@
     lax.fori_loop(0, PANELS, out, 0)
 
 
-def factor_pivots(me, shares):
+def exchange(pick, front, tiles, labels):
+    fronts = lax.axis_size("front")
+    devices = labels.shape[0]
     order = PANELS * PW
+    share = (2, PANELS // 2 * (PW // fronts), (PANELS + 1) * PW // 2)
+    box = (devices, SLOTS * TB + LABEL_ROWS, TB)
     return pl.pallas_call(
-        pivot_kernel,
-        grid_spec=pltpu.PrefetchScalarGridSpec(
-            num_scalar_prefetch=1,
-            grid=(1,),
-            in_specs=[pl.BlockSpec(memory_space=pl.ANY)],
-            out_specs=[
-                pl.BlockSpec((order, order), lambda i, m: (0, 0)),
-                pl.BlockSpec((PANELS, PW, PW), lambda i, m: (0, 0, 0)),
-                pl.BlockSpec((PW, order), lambda i, m: (0, 0)),
-            ],
-            scratch_shapes=[
-                pltpu.VMEM((order // 8, 8, order), jnp.float32),
-                pltpu.SemaphoreType.DMA,
-            ],
-        ),
+        exchange_kernel,
+        in_specs=[
+            pl.BlockSpec(memory_space=pltpu.SMEM),
+            pl.BlockSpec(memory_space=pl.ANY),
+            pl.BlockSpec(memory_space=pl.ANY),
+            pl.BlockSpec(memory_space=pltpu.VMEM),
+        ],
+        out_specs=[pl.BlockSpec(memory_space=pltpu.VMEM)] * 3
+        + [pl.BlockSpec(memory_space=pl.ANY)],
         out_shape=[
             jax.ShapeDtypeStruct((order, order), jnp.bfloat16),
             jax.ShapeDtypeStruct((PANELS, PW, PW), jnp.float32),
             jax.ShapeDtypeStruct((PW, order), jnp.float32),
+            jax.ShapeDtypeStruct(box, jnp.bfloat16),
         ],
-        compiler_params=pltpu.CompilerParams(vmem_limit_bytes=60 * MIB),
-        cost_estimate=pl.CostEstimate(
-            flops=80_000_000_000, bytes_accessed=20_000_000, transcendentals=0
+        scratch_shapes=[
+            pltpu.VMEM((order // 8, 8, order), jnp.float32),
+            pltpu.VMEM(tiles.shape, jnp.bfloat16),
+            pltpu.VMEM(box, jnp.bfloat16),
+            pltpu.VMEM(share, jnp.float32),
+            pltpu.VMEM((fronts,) + share, jnp.float32),
+            pltpu.SemaphoreType.DMA,
+            pltpu.SemaphoreType.DMA,
+            pltpu.SemaphoreType.DMA((devices,)),
+            pltpu.SemaphoreType.DMA((devices,)),
+            pltpu.SemaphoreType.DMA((9,)),
+            pltpu.SemaphoreType.DMA((2, fronts)),
+        ]
+        + RING_SEMS,
+        compiler_params=pltpu.CompilerParams(
+            collective_id=2, has_side_effects=True, vmem_limit_bytes=60 * MIB
         ),
-        name="factor_pivots",
-    )(me, shares)
-
-
-def pack_kernel(pick_ref, tiles_ref, labels_ref, outbox_ref, sem, label_sem):
-    tail = outbox_ref.shape[0] // GROUPS - PANELS
-    labels = pltpu.make_async_copy(
-        labels_ref, outbox_ref.at[:, pl.ds(SLOTS * TB, LABEL_ROWS)], label_sem
-    )
-    labels.start()
-
-    def send(i, c):
-        device = i // tail * (tail + PANELS) + PANELS + i % tail
-        for s in range(SLOTS):
-            pltpu.make_async_copy(
-                tiles_ref.at[pick_ref[device * SLOTS + s]],
-                outbox_ref.at[device, pl.ds(s * TB, TB)],
-                sem,
-            ).start()
-        return c
-
-    lax.fori_loop(0, GROUPS * tail, send, 0, unroll=4)
-    filled = outbox_ref.at[pl.ds(0, GROUPS * tail), pl.ds(0, SLOTS * TB)]
-    pltpu.make_async_copy(filled, filled, sem).wait()
-    labels.wait()
-
-
-def pack_tiles(pick, tiles, labels):
-    devices = labels.shape[0]
-    return pl.pallas_call(
-        pack_kernel,
-        grid_spec=pltpu.PrefetchScalarGridSpec(
-            num_scalar_prefetch=1,
-            grid=(1,),
-            in_specs=[
-                pl.BlockSpec(tiles.shape, lambda i, p: (0, 0, 0)),
-                pl.BlockSpec(labels.shape, lambda i, p: (0, 0, 0)),
-            ],
-            out_specs=pl.BlockSpec(memory_space=pl.ANY),
-            scratch_shapes=[pltpu.SemaphoreType.DMA, pltpu.SemaphoreType.DMA],
-        ),
-        out_shape=jax.ShapeDtypeStruct((devices, SLOTS * TB + LABEL_ROWS, TB), jnp.bfloat16),
-        compiler_params=pltpu.CompilerParams(vmem_limit_bytes=60 * MIB),
-        name="pack_tiles",
-    )(pick, tiles, labels)
+        name="exchange_and_factor",
+    )(pick, front, tiles, labels)
 
 
 CHUNK = 16
@@ -720,7 +744,6 @@
     devices = groups * fronts
     tail = fronts - PANELS
     me = lax.axis_index("front")
-    shares = spread_pivots(work)
 
     target = tile_route[0, :, 0]
     destination = target // tail * fronts + PANELS + target % tail
@@ -739,13 +762,10 @@
     labels = jnp.broadcast_to(
         labels.astype(jnp.bfloat16)[:, None, :], (devices, LABEL_ROWS, TB)
     )
-    outbox = pack_tiles(pick.reshape(devices * SLOTS), tiles, labels)
-    outbox, shares = lax.optimization_barrier((outbox, shares))
-    inbox = lax.all_to_all(outbox, ("group", "front"), 0, 0, tiled=True)
-    tags = inbox[:, SLOTS * TB, :SLOTS].astype(jnp.int32).reshape(devices * SLOTS)
-
+    bits, inverse, own, inbox = exchange(pick.reshape(devices * SLOTS), work, tiles, labels)
+    tags = jnp.where(me >= PANELS, inbox[:, SLOTS * TB, :SLOTS].astype(jnp.int32), -1)
+    tags = tags.reshape(devices * SLOTS)
     self = me.astype(jnp.int32).reshape(1)
-    bits, inverse, own = factor_pivots(self, shares)
     factor, rows, rest = solve_rows(tags, self, work, inbox, bits, inverse, own)
     schur = gather_schur(rows, rest)
     return (factor[None], schur[None])

time: 282 us -> 266 us (0.943)
  waiting for transfers between devices: 33.6 us -> 0 us
  Pallas kernels: 229 us -> 252 us
  starting transfers between devices: 7.33 us -> 0 us
    all_to_all x1 -> x0, waiting for transfers between devices: 33.6 us -> none  [on_device(): inbox = lax.all_to_all(outbox, ('group', 'front'), 0, 0, tiled=True)]
    pallas_call x3 -> x1, Pallas kernels: 128 us -> 152 us  [exchange(): pl.pallas_call(exchange_kernel, in_specs=[pl.BlockSpec(memory_space=pltpu...]
    all_to_all x1 -> x0, starting transfers between devices: 7.33 us -> none  [on_device(): inbox = lax.all_to_all(outbox, ('group', 'front'), 0, 0, tiled=True)]
    unnamed x5 -> x1, local copies, waits for them, and re-layouts: 6.28 us -> 6.27 us
  transfers between devices with their start and end apart: 1 -> 0, of which waited for: 1 -> 0; matrix products, arithmetic and copies ran while one was open for 0% -> 0% of each run, Pallas kernels for 25% -> 0%
where the time goes in v4:
time: 266 us; the launch traced here: 265 us
  Pallas kernels  252 us (95%)
  local copies, waits for them, and re-layouts  8.67 us (3%)
  other arithmetic  2.96 us (1%)
    pallas_call x1, Pallas kernels, exchange(): pl.pallas_call(exchange_kernel, in_specs=[pl.BlockSpec(memory_space=pltpu...  152 us
    pallas_call x1, Pallas kernels, gather_schur(): pl.pallas_call(schur_kernel, in_specs=[pl.BlockSpec(memory_space=pltpu.VM...  86.9 us
    pallas_call x1, Pallas kernels, solve_rows(): pl.pallas_call(solve_kernel, grid_spec=pltpu.PrefetchScalarGridSpec(num_s...  14 us
    unnamed x1, local copies, waits for them, and re-layouts  6.27 us

profile of v4, /device:TPU:1, one launch (start us, length us, event | category | flops | bytes accessed | tf_op | source)
XLA Modules:
  0.0 264.7 jit_solution(15463170453868837091)
XLA Ops:
  0.6 0.7 fusion.3
  1.3 0.7 add_bitcast_fusion
  2.0 0.1 select_reduce_fusion.3
  2.1 0.2 select_reduce_fusion.1
  2.4 0.1 select_convert_fusion
  2.5 0.1 copy.8
  2.6 0.7 reshape.114.pick_ref
  3.3 0.9 broadcast_in_dim.103.labels_ref
  4.1 151.5 %exchange_and_factor.1 = (bf16[1536,1536]{1,0:T(8,128)(2,1)}, f32[6,256,256]{2,1,0:T(8,128)}, f32[256,1536]{1,0:T(8,128)}, bf16[128,272,128]{2,1,0:T(8,128)(2,1)}) custom-call(s32[256]{0:T(256)} %reshape.114.pick_ref, f32[256,8192]{1,0:T(8,128)} %bitcast.26, bf16[128,128,128]{2,1,0:T(8,128)(2,1)} %bitcast.29, bf16[128,16,128]{2,1,0:T(8,128)(2,1)} %broadcast_in_dim.103.labels_ref), custom_call_target="tpu_custom_call" | custom-call | tf_op jit(solution)/shard_map/exchange_and_factor/pallas_call | solution.py:607
  155.7 1.2 fusion
  156.9 0.7 select_n.74.tags_ref
  157.6 14.0 %solve_rows.1 = (f32[256,1536]{1,0:T(8,128)}, bf16[256,1536]{1,0:T(8,128)(2,1)}, f32[256,6656]{1,0:T(8,128)}) custom-call(s32[256]{0:T(256)} %select_n.74.tags_ref, s32[1]{0:T(128)} %bitcast.8.me_ref, f32[256,8192]{1,0:T(8,128)} %bitcast.27, bf16[128,272,128]{2,1,0:T(8,128)(2,1)} %get-tuple-element.9.inbox_ref, ...), custom_call_target="tpu_custom_call" | custom-call | tf_op jit(solution)/shard_map/solve_rows/pallas_call | solution.py:704
  171.6 86.9 %gather_schur.1 = f32[256,6656]{1,0:T(8,128)} custom-call(bf16[256,1536]{1,0:T(8,128)(2,1)} %get-tuple-element.14.rows_ref, f32[256,6656]{1,0:T(8,128)} %get-tuple-element.15.rest_ref), custom_call_target="tpu_custom_call" | custom-call | tf_op jit(solution)/shard_map/gather_schur/pallas_call | solution.py:354
  258.5 6.3 %copy.10 = f32[1,256,6656]{2,1,0:T(8,128)} copy(f32[1,256,6656]{2,1,0:T(8,128)} %bitcast.28) | data formatting | bytes 13631488
  (5 shorter events, 0.0 us)

commit v5 on v4

--- a/solution.py
+++ b/solution.py
@@ -12,7 +12,6 @@
 TB = 128
 SUB = 16
 SLOTS = 2
-LABEL_ROWS = 16
 AHEAD = 4
 EARLY = 10
 EACH = 1
@@ -365,7 +364,7 @@
         ]
         + RING_SEMS,
         compiler_params=pltpu.CompilerParams(
-            collective_id=1, has_side_effects=True, vmem_limit_bytes=60 * MIB
+            collective_id=1, has_side_effects=True, vmem_limit_bytes=40 * MIB
         ),
         name="gather_schur",
     )(rows, rest)
@@ -443,9 +442,10 @@
 
 def exchange_kernel(
     pick_ref, front_ref, tiles_ref, labels_ref,
-    bits_ref, inverse_ref, own_ref, inbox_ref,
-    work, tiles, outbox, share, shares,
-    tile_sem, unpack_sem, ship_send, ship_recv, deal_recv, deal_send, *sems,
+    bits_out, inverse_out, own_out, inbox_ref, tags_ref,
+    bits_ref, inverse_ref, own_ref, work, tiles, outbox, share, shares,
+    tile_sem, unpack_sem, out_sems, ship_send, ship_recv, label_send, label_recv,
+    deal_recv, deal_send, *sems,
 ):
     devices = inbox_ref.shape[0]
     fronts = shares.shape[0]
@@ -476,29 +476,44 @@
         device = i // tail * fronts + PANELS + i % tail
         for s in range(SLOTS):
             outbox[device, s * TB : (s + 1) * TB] = tiles[pick_ref[device * SLOTS + s]]
-        outbox[device, SLOTS * TB :] = labels_ref[device]
         return c
 
     lax.fori_loop(0, devices // fronts * tail, pack, 0)
     def ship(k):
         device = (mine + k * 37) % devices
-        return device, pltpu.make_async_remote_copy(
-            src_ref=outbox.at[device],
-            dst_ref=inbox_ref.at[mine],
-            send_sem=ship_send.at[k],
-            recv_sem=ship_recv.at[k],
-            device_id=where_is(device),
-            device_id_type=MESH,
-        )
+        return device % fronts >= PANELS, [
+            pltpu.make_async_remote_copy(
+                src_ref=source.at[device],
+                dst_ref=target.at[mine],
+                send_sem=send_sem.at[k],
+                recv_sem=recv_sem.at[k],
+                device_id=where_is(device),
+                device_id_type=MESH,
+            )
+            for source, target, send_sem, recv_sem in (
+                (outbox, inbox_ref, ship_send, ship_recv),
+                (labels_ref, tags_ref, label_send, label_recv),
+            )
+        ]
 
     def start(k, c):
-        device, copy = ship(k)
-        pl.when(device % fronts >= PANELS)(copy.start)
+        live, copies = ship(k)
+
+        @pl.when(live)
+        def _():
+            for copy in copies:
+                copy.start()
+
         return c
 
     def left(k, c):
-        device, copy = ship(k)
-        pl.when(device % fronts >= PANELS)(copy.wait_send)
+        live, copies = ship(k)
+
+        @pl.when(live)
+        def _():
+            for copy in copies:
+                copy.wait_send()
+
         return c
 
     def pace(k, c):
@@ -517,9 +532,16 @@
     begun = begun + STEPS * EACH
 
     lax.fori_loop(begun, devices, start, 0)
-    keep = pltpu.make_async_copy(outbox.at[mine], inbox_ref.at[mine], ship_recv.at[0])
     below = me >= PANELS
-    pl.when(below)(keep.start)
+    keep = [
+        pltpu.make_async_copy(outbox.at[mine], inbox_ref.at[mine], ship_recv.at[0]),
+        pltpu.make_async_copy(labels_ref.at[mine], tags_ref.at[mine], label_recv.at[0]),
+    ]
+
+    @pl.when(below)
+    def _():
+        for copy in keep:
+            copy.start()
 
     for i in range(PANELS):
         for half, group, source, target, width in share_segments(i):
@@ -531,15 +553,35 @@
     pltpu.make_async_copy(shares, shares, unpack_sem).wait()
     factor_pivots(me, work, bits_ref, inverse_ref, own_ref)
 
-    pl.when(below)(keep.wait)
+    results = [
+        pltpu.make_async_copy(value, target, out_sems.at[i])
+        for i, (value, target) in enumerate(
+            ((bits_ref, bits_out), (inverse_ref, inverse_out), (own_ref, own_out))
+        )
+    ]
+    for copy in results:
+        copy.start()
+
+    @pl.when(below)
+    def _():
+        for copy in keep:
+            copy.wait()
 
     def landed(k, c):
-        pl.when(below)(ship(k)[1].wait_recv)
+        _, copies = ship(k)
+
+        @pl.when(below)
+        def _():
+            for copy in copies:
+                copy.wait_recv()
+
         return c
 
     lax.fori_loop(begun - AHEAD, devices, left, 0)
     lax.fori_loop(1, devices, landed, 0)
     wait_sent()
+    for copy in results:
+        copy.wait()
 
 
 def factor_pivots(me, work, bits_ref, inverse_ref, own_ref):
@@ -603,7 +645,7 @@
     devices = labels.shape[0]
     order = PANELS * PW
     share = (2, PANELS // 2 * (PW // fronts), (PANELS + 1) * PW // 2)
-    box = (devices, SLOTS * TB + LABEL_ROWS, TB)
+    box = (devices, SLOTS * TB, TB)
     return pl.pallas_call(
         exchange_kernel,
         in_specs=[
@@ -612,15 +654,18 @@
             pl.BlockSpec(memory_space=pl.ANY),
             pl.BlockSpec(memory_space=pltpu.VMEM),
         ],
-        out_specs=[pl.BlockSpec(memory_space=pltpu.VMEM)] * 3
-        + [pl.BlockSpec(memory_space=pl.ANY)],
+        out_specs=[pl.BlockSpec(memory_space=pl.ANY)] * 5,
         out_shape=[
             jax.ShapeDtypeStruct((order, order), jnp.bfloat16),
             jax.ShapeDtypeStruct((PANELS, PW, PW), jnp.float32),
             jax.ShapeDtypeStruct((PW, order), jnp.float32),
             jax.ShapeDtypeStruct(box, jnp.bfloat16),
+            jax.ShapeDtypeStruct(labels.shape, jnp.int32),
         ],
         scratch_shapes=[
+            pltpu.VMEM((order, order), jnp.bfloat16),
+            pltpu.VMEM((PANELS, PW, PW), jnp.float32),
+            pltpu.VMEM((PW, order), jnp.float32),
             pltpu.VMEM((order // 8, 8, order), jnp.float32),
             pltpu.VMEM(tiles.shape, jnp.bfloat16),
             pltpu.VMEM(box, jnp.bfloat16),
@@ -628,6 +673,9 @@
             pltpu.VMEM((fronts,) + share, jnp.float32),
             pltpu.SemaphoreType.DMA,
             pltpu.SemaphoreType.DMA,
+            pltpu.SemaphoreType.DMA((3,)),
+            pltpu.SemaphoreType.DMA((devices,)),
+            pltpu.SemaphoreType.DMA((devices,)),
             pltpu.SemaphoreType.DMA((devices,)),
             pltpu.SemaphoreType.DMA((devices,)),
             pltpu.SemaphoreType.DMA((9,)),
@@ -645,8 +693,9 @@
 
 
 def solve_kernel(
-    tags_ref, me_ref, front_ref, inbox_ref, bits_ref, inverse_ref, own_ref,
-    factor_ref, rows_ref, rest_ref, work, landed, sems, rest_sem,
+    tags_ref, me_ref, front_ref, inbox_ref, bits_in, inverse_in, own_in,
+    factor_ref, rows_ref, rest_ref,
+    work, landed, bits_ref, inverse_ref, own_ref, sems, rest_sem, late_sems,
 ):
     pivots = PANELS * PW
     count = inbox_ref.shape[0]
@@ -662,6 +711,14 @@
 
     for c in range(chunks):
         fetch(c).start()
+    late = [
+        pltpu.make_async_copy(value, target, late_sems.at[i])
+        for i, (value, target) in enumerate(
+            ((bits_in, bits_ref), (inverse_in, inverse_ref), (own_in, own_ref))
+        )
+    ]
+    for copy in late:
+        copy.start()
     fill.wait()
 
     for c in range(chunks):
@@ -684,6 +741,8 @@
         lax.fori_loop(c * CHUNK, (c + 1) * CHUNK, add, 0)
     leave = pltpu.make_async_copy(work.at[:, pl.ds(pivots, rest_ref.shape[1])], rest_ref, rest_sem)
     leave.start()
+    for copy in late:
+        copy.wait()
     below = me_ref[0] >= PANELS
     for k in range(PANELS):
         at = slice(k * PW, (k + 1) * PW)
@@ -706,13 +765,7 @@
         grid_spec=pltpu.PrefetchScalarGridSpec(
             num_scalar_prefetch=2,
             grid=(1,),
-            in_specs=[
-                pl.BlockSpec(memory_space=pl.ANY),
-                pl.BlockSpec(memory_space=pl.ANY),
-                whole(bits.shape),
-                whole(inverse.shape),
-                whole(own.shape),
-            ],
+            in_specs=[pl.BlockSpec(memory_space=pl.ANY)] * 5,
             out_specs=[
                 whole((PW, pivots)),
                 whole((PW, pivots)),
@@ -721,8 +774,12 @@
             scratch_shapes=[
                 pltpu.VMEM((PW, order), jnp.float32),
                 pltpu.VMEM((count, SLOTS * TB, TB), jnp.bfloat16),
+                pltpu.VMEM(bits.shape, bits.dtype),
+                pltpu.VMEM(inverse.shape, inverse.dtype),
+                pltpu.VMEM(own.shape, own.dtype),
                 pltpu.SemaphoreType.DMA((count // CHUNK + 1,)),
                 pltpu.SemaphoreType.DMA,
+                pltpu.SemaphoreType.DMA((3,)),
             ],
         ),
         out_shape=[
@@ -730,7 +787,7 @@
             jax.ShapeDtypeStruct((PW, pivots), jnp.bfloat16),
             jax.ShapeDtypeStruct((PW, order - pivots), jnp.float32),
         ],
-        compiler_params=pltpu.CompilerParams(vmem_limit_bytes=60 * MIB),
+        compiler_params=pltpu.CompilerParams(vmem_limit_bytes=34 * MIB),
         name="solve_rows",
     )(tags, me, front, inbox, bits, inverse, own)
 
@@ -758,13 +815,11 @@
     here = (positions[None, :] == last[:, None]) & (last != first)[:, None]
     label_last = jnp.max(jnp.where(here, label[None, :], -1), axis=1)
     lane = jnp.arange(TB, dtype=jnp.int32)[None, :]
-    labels = jnp.where(lane == 0, label_first[:, None], label_last[:, None])
-    labels = jnp.broadcast_to(
-        labels.astype(jnp.bfloat16)[:, None, :], (devices, LABEL_ROWS, TB)
+    labels = jnp.where(lane == 0, label_first[:, None], label_last[:, None])[:, None, :]
+    bits, inverse, own, inbox, tags = exchange(
+        pick.reshape(devices * SLOTS), work, tiles, labels
     )
-    bits, inverse, own, inbox = exchange(pick.reshape(devices * SLOTS), work, tiles, labels)
-    tags = jnp.where(me >= PANELS, inbox[:, SLOTS * TB, :SLOTS].astype(jnp.int32), -1)
-    tags = tags.reshape(devices * SLOTS)
+    tags = jnp.where(me >= PANELS, tags[:, 0, :SLOTS], -1).reshape(devices * SLOTS)
     self = me.astype(jnp.int32).reshape(1)
     factor, rows, rest = solve_rows(tags, self, work, inbox, bits, inverse, own)
     schur = gather_schur(rows, rest)

time: 266 us -> 253 us (0.951)
  Pallas kernels: 252 us -> 238 us
    pallas_call x1, Pallas kernels: 152 us -> 145 us  [exchange(): pl.pallas_call(exchange_kernel, in_specs=[pl.BlockSpec(memory_space=pltpu...]
    pallas_call x1, Pallas kernels: 86.9 us -> 82.6 us  [gather_schur(): pl.pallas_call(schur_kernel, in_specs=[pl.BlockSpec(memory_space=pltpu.VM...]
    pallas_call x1, Pallas kernels: 14 us -> 10.4 us  [solve_rows(): pl.pallas_call(solve_kernel, grid_spec=pltpu.PrefetchScalarGridSpec(num_s...]
    unnamed x1 -> x7, local copies, waits for them, and re-layouts: 6.27 us -> 8.03 us
where the time goes in v5:
time: 253 us; the launch traced here: 251 us
  Pallas kernels  238 us (94%)
  local copies, waits for them, and re-layouts  8.98 us (4%)
  other arithmetic  3.68 us (1%)
    pallas_call x1, Pallas kernels, exchange(): pl.pallas_call(exchange_kernel, in_specs=[pl.BlockSpec(memory_space=pltpu...  145 us
    pallas_call x1, Pallas kernels, gather_schur(): pl.pallas_call(schur_kernel, in_specs=[pl.BlockSpec(memory_space=pltpu.VM...  82.6 us
    pallas_call x1, Pallas kernels, solve_rows(): pl.pallas_call(solve_kernel, grid_spec=pltpu.PrefetchScalarGridSpec(num_s...  10.4 us
    unnamed x7, local copies, waits for them, and re-layouts  8.03 us

profile of v5, /device:TPU:1, one launch (start us, length us, event | category | flops | bytes accessed | tf_op | source)
XLA Modules:
  0.0 251.1 jit_solution(4870529371496608060)
XLA Ops:
  0.6 0.7 fusion.3
  1.3 0.7 add_bitcast_fusion
  2.0 0.1 select_reduce_fusion.3
  2.1 0.2 select_reduce_fusion.1
  2.4 1.0 broadcast_select_fusion.labels_ref
  3.3 0.1 copy.8
  3.4 0.7 reshape.135.pick_ref
  4.1 144.7 %exchange_and_factor.1 = (bf16[1536,1536]{1,0:T(8,128)(2,1)}, f32[6,256,256]{2,1,0:T(8,128)}, f32[256,1536]{1,0:T(8,128)}, bf16[128,256,128]{2,1,0:T(8,128)(2,1)}, s32[128,1,128]{2,1,0:T(1,128)}) custom-call(s32[256]{0:T(256)} %reshape.135.pick_ref, f32[256,8192]{1,0:T(8,128)} %bitcast.27, bf16[128,128,128]{2,1,0:T(8,128)(2,1)} %bitcast.29, ...), custom_call_target="tpu_custom_call" | custom-call | tf_op jit(solution)/shard_map/exchange_and_factor/pallas_call | solution.py:649
  148.9 1.0 fusion
  149.9 0.1 select_n.77.tags_ref
  150.1 0.0 copy-start
  150.1 2.3 copy-done
  152.4 0.0 copy-start.1
  152.4 1.4 copy-done.1
  153.8 0.0 copy-start.2
  153.8 1.4 copy-done.2
  155.2 10.4 %solve_rows.1 = (f32[256,1536]{1,0:T(8,128)}, bf16[256,1536]{1,0:T(8,128)(2,1)S(1)}, f32[256,6656]{1,0:T(8,128)S(1)}) custom-call(s32[256]{0:T(256)S(1)} %select_n.77.tags_ref, s32[1]{0:T(128)} %bitcast.8.me_ref, f32[256,8192]{1,0:T(8,128)} %bitcast.28, bf16[128,256,128]{2,1,0:T(8,128)(2,1)} %get-tuple-element.11.inbox_ref, bf16[1536,1536]{1,0:T(8,128)(2,1)S(1)} %copy-done, ...), custom_call_target="tpu_custom_call" | custom-call | tf_op jit(solution)/shard_map/solve_rows/pallas_call | solution.py:763
  165.6 82.6 %gather_schur.1 = f32[256,6656]{1,0:T(8,128)S(1)} custom-call(bf16[256,1536]{1,0:T(8,128)(2,1)S(1)} %get-tuple-element.16.rows_ref, f32[256,6656]{1,0:T(8,128)S(1)} %get-tuple-element.17.rest_ref), custom_call_target="tpu_custom_call" | custom-call | tf_op jit(solution)/shard_map/gather_schur/pallas_call | solution.py:353
  248.2 2.9 %copy.10 = f32[1,256,6656]{2,1,0:T(8,128)} copy(f32[1,256,6656]{2,1,0:T(8,128)S(1)} %bitcast.26) | data formatting | bytes 13631488
  (5 shorter events, 0.0 us)
Async XLA Ops:
  150.1 2.3 copy-start
  152.4 1.4 copy-start.1
  153.8 1.4 copy-start.2

commit v6 on v5

--- a/solution.py
+++ b/solution.py
@@ -113,17 +113,13 @@
     return jnp.concatenate(upper, axis=0), jnp.concatenate(inverse, axis=0)
 
 
-def share_segments(i):
-    half_width = (PANELS + 1) * PW // 2
-    group = min(i, PANELS - 1 - i)
-    begin = 0 if i < PANELS // 2 else (group + 1) * PW
-    end = begin + (i + 1) * PW
-    found = []
-    for half in range(2):
-        low, high = max(begin, half * half_width), min(end, (half + 1) * half_width)
-        if low < high:
-            found.append((half, group, low - half * half_width, low - begin, high - low))
-    return found
+PLACES = {0: (1, 1, 5 * PW), 1: (0, 1, 4 * PW), 2: (0, 1, 0), 3: (1, 1, 0), 4: (1, 0, 0), 5: (0, 0, 0)}
+PART = (PANELS + 1) * PW
+SHARE_ROWS = 16
+
+
+def sent_width(i):
+    return PART if i == 4 else (i + 2) * PW
 
 
 MESH = pl.DeviceIdType.MESH
@@ -169,13 +165,15 @@
             pl.semaphore_signal(barrier, inc=1, device_id={"front": peer}, device_id_type=MESH)
         return barrier
 
-    def gather(self, own, out, sems, after=None, taken=False):
+    def gather(self, own, out, sems, after=None, taken=False, whole=False):
         ring_recv, side_recv, own_recv, local_sem, send_sem = sems
         core = self.core
 
         def piece(da, db, s, other=False):
             half = 1 - core if other else core
             chip = self.chip(da, db, other)
+            if whole:
+                return out.at[half, chip] if s is None else out.at[half, chip, s]
             if s is None:
                 return out.at[pl.ds(2 * chip, 2), half]
             return out.at[2 * chip + s, half]
@@ -220,14 +218,17 @@
             remote(ref, ref, recv, to, self.live(da, db))
 
         here = self.live(0, 0)
-        mine = pltpu.make_async_copy(own(core), piece(0, 0, core), local_sem.at[0])
-        rest = pltpu.make_async_copy(own(1 - core), piece(0, 0, core, True), local_sem.at[1])
-        when(here, mine.start)
-        when(here, rest.start)
-        remote(own(1 - core), piece(0, 0, core, True), own_recv.at[0], "s", here)
-        remote(own(core), piece(0, 0, core), own_recv.at[1], "s", here)
-        when(here, mine.wait)
-        arrive(piece(0, 0, 1 - core), own_recv.at[0], here)
+        if whole:
+            give(0, 0, None, "s")
+        else:
+            mine = pltpu.make_async_copy(own(core), piece(0, 0, core), local_sem.at[0])
+            rest = pltpu.make_async_copy(own(1 - core), piece(0, 0, core, True), local_sem.at[1])
+            when(here, mine.start)
+            when(here, rest.start)
+            remote(own(1 - core), piece(0, 0, core, True), own_recv.at[0], "s", here)
+            remote(own(core), piece(0, 0, core), own_recv.at[1], "s", here)
+            when(here, mine.wait)
+            arrive(piece(0, 0, 1 - core), own_recv.at[0], here)
         for to in MOVES:
             give(0, 0, None, to)
         steps = [
@@ -255,6 +256,8 @@
             (2, 2, 1, []),
         ]
         def take_own():
+            if whole:
+                return arrive(piece(0, 0, None, True), side_recv.at[0, 0, 0], here)
             arrive(piece(0, 0, 1 - core, True), own_recv.at[1], here)
             when(here, rest.wait)
 
@@ -370,65 +373,77 @@
     )(rows, rest)
 
 
-def deal_shares(ring, front_ref, share, deal_recv, deal_send, fronts):
+def round_rows(me, staged, rounded):
+    for i in range(PANELS):
+
+        @pl.when(me == i)
+        def _():
+            width = (i + 1) * PW
+            rounded[:, :width] = staged[:, :width].astype(jnp.bfloat16)
+            diagonal = staged[:, i * PW : width]
+            taken = diagonal - diagonal.astype(jnp.bfloat16).astype(jnp.float32)
+            rounded[:, width : width + PW] = taken.astype(jnp.bfloat16)
+            if sent_width(i) > width + PW:
+                rounded[:, width + PW :] = jnp.zeros((PW, PW), jnp.bfloat16)
+
+
+def deal_shares(ring, rounded, shares, deal_recv, deal_send):
     me = ring.me
-    pieces = []
-    for i in range(PANELS):
-        for segment in share_segments(i):
-            pieces.append((i, len(pieces)) + segment)
-
-    def source(f, piece):
-        i, _, _, _, _, column, width = piece
-        return front_ref.at[pl.ds(pl.multiple_of(f * 8, 8), 8), pl.ds(column, width)]
-
-    def target(piece):
-        _, _, half, group, column, _, width = piece
-        return share.at[half, pl.ds(group * 8, 8), pl.ds(column, width)]
-
-    def far(f, piece):
+    chips = shares.shape[1]
+
+    def ends(i, chip):
+        half, part, first = PLACES[i]
+        rows = pl.ds(pl.multiple_of(chip * SHARE_ROWS, SHARE_ROWS), SHARE_ROWS)
+        return (
+            rounded.at[rows, pl.ds(0, sent_width(i))],
+            shares.at[half, chip, part, :, pl.ds(first, sent_width(i))],
+        )
+
+    def far(i, chip):
+        source, target = ends(i, chip)
         return pltpu.make_async_remote_copy(
-            src_ref=source(f, piece),
-            dst_ref=target(piece),
-            send_sem=deal_send.at[piece[2], f],
-            recv_sem=deal_recv.at[piece[1]],
-            device_id={"front": f},
+            src_ref=source,
+            dst_ref=target,
+            send_sem=deal_send.at[chip],
+            recv_sem=deal_recv.at[i],
+            device_id={"front": 2 * chip + PLACES[i][0]},
             device_id_type=MESH,
         )
 
-    def near(piece):
-        return pltpu.make_async_copy(source(me, piece), target(piece), deal_recv.at[piece[1]])
+    def near(i):
+        return pltpu.make_async_copy(*ends(i, me // 2), deal_recv.at[i])
 
     def each(i, action):
-        mine = [piece for piece in pieces if piece[0] == i]
-
-        def one(f, c):
-            @pl.when(f != me)
+        def one(chip, c):
+            @pl.when(2 * chip + PLACES[i][0] != me)
             def _():
-                for piece in mine:
-                    action(far(f, piece))
+                action(far(i, chip))
 
             return c
 
-        lax.fori_loop(0, fronts, one, 0)
-        return mine
+        lax.fori_loop(0, chips, one, 0)
 
     for i in range(PANELS):
 
         @pl.when(me == i)
         def _():
-            for piece in each(i, lambda copy: copy.start()):
-                near(piece).start()
+            each(i, lambda copy: copy.start())
+            if PLACES[i][0] == i % 2:
+                near(i).start()
 
     def wait_share():
-        for piece in pieces:
-
-            @pl.when(me == piece[0])
+        for i in range(PANELS):
+            takes = ring.core == PLACES[i][0]
+
+            @pl.when(takes & (me != i))
             def _():
-                near(piece).wait()
-
-            @pl.when(me != piece[0])
-            def _():
-                far(0, piece).wait_recv()
+                far(i, me // 2).wait_recv()
+
+            if PLACES[i][0] == i % 2:
+
+                @pl.when(me == i)
+                def _():
+                    near(i).wait()
 
     def wait_sent():
         for i in range(PANELS):
@@ -443,18 +458,20 @@
 def exchange_kernel(
     pick_ref, front_ref, tiles_ref, labels_ref,
     bits_out, inverse_out, own_out, inbox_ref, tags_ref,
-    bits_ref, inverse_ref, own_ref, work, tiles, outbox, share, shares,
-    tile_sem, unpack_sem, out_sems, ship_send, ship_recv, label_send, label_recv,
+    bits_ref, inverse_ref, own_ref, work, tiles, outbox, staged, rounded, shares,
+    tile_sem, stage_sem, out_sems, ship_send, ship_recv, label_send, label_recv,
     deal_recv, deal_send, *sems,
 ):
     devices = inbox_ref.shape[0]
-    fronts = shares.shape[0]
+    fronts = 2 * shares.shape[1]
     tail = fronts - PANELS
     ring = Ring(0)
     me = ring.me
     mine = lax.axis_index("group") * fronts + me
     fetch = pltpu.make_async_copy(tiles_ref, tiles, tile_sem)
     fetch.start()
+    stage = pltpu.make_async_copy(front_ref.at[:, pl.ds(0, PANELS * PW)], staged, stage_sem)
+    pl.when(me < PANELS)(stage.start)
 
     def where_is(device):
         return {"group": device // fronts, "front": device % fronts}
@@ -467,8 +484,10 @@
         return c
 
     lax.fori_loop(1, devices, greet, 0)
+    pl.when(me < PANELS)(stage.wait)
+    round_rows(me, staged, rounded)
     pl.semaphore_wait(barrier, devices - 1)
-    wait_share, wait_sent = deal_shares(ring, front_ref, share, deal_recv, deal_send, fronts)
+    wait_share, wait_sent = deal_shares(ring, rounded, shares, deal_recv, deal_send)
 
     fetch.wait()
 
@@ -480,7 +499,7 @@
 
     lax.fori_loop(0, devices // fronts * tail, pack, 0)
     def ship(k):
-        device = (mine + k * 37) % devices
+        device = (mine + k * 59) % devices
         return device % fronts >= PANELS, [
             pltpu.make_async_remote_copy(
                 src_ref=source.at[device],
@@ -528,7 +547,7 @@
         lax.fori_loop(begun + step * EACH, begun + (step + 1) * EACH, pace, 0)
 
     wait_share()
-    ring.gather(lambda h: share.at[h], shares, sems, after)
+    ring.gather(None, shares, sems, after, whole=True)
     begun = begun + STEPS * EACH
 
     lax.fori_loop(begun, devices, start, 0)
@@ -543,14 +562,21 @@
         for copy in keep:
             copy.start()
 
-    for i in range(PANELS):
-        for half, group, source, target, width in share_segments(i):
-            pltpu.make_async_copy(
-                shares.at[:, half, pl.ds(group * 8, 8), pl.ds(source, width)],
-                work.at[pl.ds(i * fronts, fronts), :, pl.ds(target, width)],
-                unpack_sem,
-            ).start()
-    pltpu.make_async_copy(shares, shares, unpack_sem).wait()
+    def unpack(chip, c):
+        for i in range(PANELS):
+            half, part, first = PLACES[i]
+            width = (i + 1) * PW
+            rows = pl.ds(i * fronts + 2 * chip, 2)
+
+            def take(start, count):
+                value = shares[half, chip, part, :, start : start + count].astype(jnp.float32)
+                return value.reshape(2, 8, count)
+
+            work[rows, :, :width] = take(first, width)
+            work[rows, :, i * PW : width] += take(first + width, PW)
+        return c
+
+    lax.fori_loop(0, fronts // 2, unpack, 0)
     factor_pivots(me, work, bits_ref, inverse_ref, own_ref)
 
     results = [
@@ -644,7 +670,6 @@
     fronts = lax.axis_size("front")
     devices = labels.shape[0]
     order = PANELS * PW
-    share = (2, PANELS // 2 * (PW // fronts), (PANELS + 1) * PW // 2)
     box = (devices, SLOTS * TB, TB)
     return pl.pallas_call(
         exchange_kernel,
@@ -669,8 +694,9 @@
             pltpu.VMEM((order // 8, 8, order), jnp.float32),
             pltpu.VMEM(tiles.shape, jnp.bfloat16),
             pltpu.VMEM(box, jnp.bfloat16),
-            pltpu.VMEM(share, jnp.float32),
-            pltpu.VMEM((fronts,) + share, jnp.float32),
+            pltpu.VMEM((PW, order), jnp.float32),
+            pltpu.VMEM((PW, PART), jnp.bfloat16),
+            pltpu.VMEM((2, fronts // 2, 2, SHARE_ROWS, PART), jnp.bfloat16),
             pltpu.SemaphoreType.DMA,
             pltpu.SemaphoreType.DMA,
             pltpu.SemaphoreType.DMA((3,)),
@@ -678,8 +704,8 @@
             pltpu.SemaphoreType.DMA((devices,)),
             pltpu.SemaphoreType.DMA((devices,)),
             pltpu.SemaphoreType.DMA((devices,)),
-            pltpu.SemaphoreType.DMA((9,)),
-            pltpu.SemaphoreType.DMA((2, fronts)),
+            pltpu.SemaphoreType.DMA((PANELS,)),
+            pltpu.SemaphoreType.DMA((fronts // 2,)),
         ]
         + RING_SEMS,
         compiler_params=pltpu.CompilerParams(

time: 253 us -> 244 us (0.964)
  Pallas kernels: 238 us -> 229 us
    pallas_call x1, Pallas kernels: 145 us -> 136 us  [exchange(): pl.pallas_call(exchange_kernel, in_specs=[pl.BlockSpec(memory_space=pltpu...]
where the time goes in v6:
time: 244 us; the launch traced here: 243 us
  Pallas kernels  229 us (94%)
  local copies, waits for them, and re-layouts  8.98 us (4%)
  other arithmetic  3.68 us (2%)
    pallas_call x1, Pallas kernels, exchange(): pl.pallas_call(exchange_kernel, in_specs=[pl.BlockSpec(memory_space=pltpu...  136 us
    pallas_call x1, Pallas kernels, gather_schur(): pl.pallas_call(schur_kernel, in_specs=[pl.BlockSpec(memory_space=pltpu.VM...  82.7 us
    pallas_call x1, Pallas kernels, solve_rows(): pl.pallas_call(solve_kernel, grid_spec=pltpu.PrefetchScalarGridSpec(num_s...  10.4 us
    unnamed x7, local copies, waits for them, and re-layouts  8.03 us

profile of v6, /device:TPU:1, one launch (start us, length us, event | category | flops | bytes accessed | tf_op | source)
XLA Modules:
  0.0 242.7 jit_solution(1693702467458220950)
XLA Ops:
  0.6 0.7 fusion.3
  1.3 0.7 add_bitcast_fusion
  2.0 0.1 select_reduce_fusion.3
  2.1 0.2 select_reduce_fusion.1
  2.4 1.0 broadcast_select_fusion.labels_ref
  3.3 0.1 copy.8
  3.4 0.7 reshape.135.pick_ref
  4.1 136.2 %exchange_and_factor.1 = (bf16[1536,1536]{1,0:T(8,128)(2,1)}, f32[6,256,256]{2,1,0:T(8,128)}, f32[256,1536]{1,0:T(8,128)}, bf16[128,256,128]{2,1,0:T(8,128)(2,1)}, s32[128,1,128]{2,1,0:T(1,128)}) custom-call(s32[256]{0:T(256)} %reshape.135.pick_ref, f32[256,8192]{1,0:T(8,128)} %bitcast.27, bf16[128,128,128]{2,1,0:T(8,128)(2,1)} %bitcast.29, ...), custom_call_target="tpu_custom_call" | custom-call | tf_op jit(solution)/shard_map/exchange_and_factor/pallas_call | solution.py:674
  140.4 1.0 fusion
  141.4 0.1 select_n.77.tags_ref
  141.6 0.0 copy-start
  141.6 2.3 copy-done
  143.9 0.0 copy-start.1
  143.9 1.4 copy-done.1
  145.3 0.0 copy-start.2
  145.3 1.4 copy-done.2
  146.7 10.4 %solve_rows.1 = (f32[256,1536]{1,0:T(8,128)}, bf16[256,1536]{1,0:T(8,128)(2,1)S(1)}, f32[256,6656]{1,0:T(8,128)S(1)}) custom-call(s32[256]{0:T(256)S(1)} %select_n.77.tags_ref, s32[1]{0:T(128)} %bitcast.8.me_ref, f32[256,8192]{1,0:T(8,128)} %bitcast.28, bf16[128,256,128]{2,1,0:T(8,128)(2,1)} %get-tuple-element.11.inbox_ref, bf16[1536,1536]{1,0:T(8,128)(2,1)S(1)} %copy-done, ...), custom_call_target="tpu_custom_call" | custom-call | tf_op jit(solution)/shard_map/solve_rows/pallas_call | solution.py:789
  157.1 82.7 %gather_schur.1 = f32[256,6656]{1,0:T(8,128)S(1)} custom-call(bf16[256,1536]{1,0:T(8,128)(2,1)S(1)} %get-tuple-element.16.rows_ref, f32[256,6656]{1,0:T(8,128)S(1)} %get-tuple-element.17.rest_ref), custom_call_target="tpu_custom_call" | custom-call | tf_op jit(solution)/shard_map/gather_schur/pallas_call | solution.py:356
  239.8 2.9 %copy.10 = f32[1,256,6656]{2,1,0:T(8,128)} copy(f32[1,256,6656]{2,1,0:T(8,128)S(1)} %bitcast.26) | data formatting | bytes 13631488
  (5 shorter events, 0.0 us)
Async XLA Ops:
  141.6 2.3 copy-start
  143.9 1.4 copy-start.1
  145.3 1.4 copy-start.2

commit v7 on v6

--- a/solution.py
+++ b/solution.py
@@ -287,7 +287,7 @@
     (0, 0), (0, 3), (0, 1), (3, 0), (1, 0), (0, 2), (3, 3), (1, 3),
     (3, 1), (1, 1), (2, 0), (3, 2), (1, 2), (2, 3), (2, 1), (2, 2),
 ]
-BATCHES = {5: (0, 6, 0, 5), 9: (6, 10, 5, 8), 11: (10, 11, 8, 10), 15: (11, 13, 10, 11), 21: (13, 16, 11, 16)}
+BATCHES = {5: (0, 6, 0, 5), 9: (6, 10, 5, 8), 11: (10, 11, 8, 10), 15: (11, 13, 10, 11), 17: (13, 14, 11, 12), 19: (14, 15, 12, 13), 21: (15, 16, 13, 16)}
 
 
 RING_SEMS = [

time: 244 us -> 242 us (level)
  no operation moved by 1% of the time
where the time goes in v7:
time: 242 us
  Pallas kernels  228 us (94%)
  local copies, waits for them, and re-layouts  8.98 us (4%)
  other arithmetic  3.68 us (2%)
    pallas_call x1, Pallas kernels, exchange(): pl.pallas_call(exchange_kernel, in_specs=[pl.BlockSpec(memory_space=pltpu...  136 us
    pallas_call x1, Pallas kernels, gather_schur(): pl.pallas_call(schur_kernel, in_specs=[pl.BlockSpec(memory_space=pltpu.VM...  81.6 us
    pallas_call x1, Pallas kernels, solve_rows(): pl.pallas_call(solve_kernel, grid_spec=pltpu.PrefetchScalarGridSpec(num_s...  10.4 us
    unnamed x7, local copies, waits for them, and re-layouts  8.03 us

profile of v7, /device:TPU:1, one launch (start us, length us, event | category | flops | bytes accessed | tf_op | source)
XLA Modules:
  0.0 241.6 jit_solution(10123332809860338461)
XLA Ops:
  0.6 0.7 fusion.3
  1.3 0.7 add_bitcast_fusion
  2.0 0.1 select_reduce_fusion.3
  2.1 0.2 select_reduce_fusion.1
  2.4 1.0 broadcast_select_fusion.labels_ref
  3.3 0.1 copy.8
  3.4 0.7 reshape.135.pick_ref
  4.1 136.2 %exchange_and_factor.1 = (bf16[1536,1536]{1,0:T(8,128)(2,1)}, f32[6,256,256]{2,1,0:T(8,128)}, f32[256,1536]{1,0:T(8,128)}, bf16[128,256,128]{2,1,0:T(8,128)(2,1)}, s32[128,1,128]{2,1,0:T(1,128)}) custom-call(s32[256]{0:T(256)} %reshape.135.pick_ref, f32[256,8192]{1,0:T(8,128)} %bitcast.27, bf16[128,128,128]{2,1,0:T(8,128)(2,1)} %bitcast.29, ...), custom_call_target="tpu_custom_call" | custom-call | tf_op jit(solution)/shard_map/exchange_and_factor/pallas_call | solution.py:674
  140.4 1.0 fusion
  141.4 0.1 select_n.77.tags_ref
  141.6 0.0 copy-start
  141.6 2.3 copy-done
  143.9 0.0 copy-start.1
  143.9 1.4 copy-done.1
  145.3 0.0 copy-start.2
  145.3 1.4 copy-done.2
  146.7 10.4 %solve_rows.1 = (f32[256,1536]{1,0:T(8,128)}, bf16[256,1536]{1,0:T(8,128)(2,1)S(1)}, f32[256,6656]{1,0:T(8,128)S(1)}) custom-call(s32[256]{0:T(256)S(1)} %select_n.77.tags_ref, s32[1]{0:T(128)} %bitcast.8.me_ref, f32[256,8192]{1,0:T(8,128)} %bitcast.28, bf16[128,256,128]{2,1,0:T(8,128)(2,1)} %get-tuple-element.11.inbox_ref, bf16[1536,1536]{1,0:T(8,128)(2,1)S(1)} %copy-done, ...), custom_call_target="tpu_custom_call" | custom-call | tf_op jit(solution)/shard_map/solve_rows/pallas_call | solution.py:789
  157.1 81.6 %gather_schur.1 = f32[256,6656]{1,0:T(8,128)S(1)} custom-call(bf16[256,1536]{1,0:T(8,128)(2,1)S(1)} %get-tuple-element.16.rows_ref, f32[256,6656]{1,0:T(8,128)S(1)} %get-tuple-element.17.rest_ref), custom_call_target="tpu_custom_call" | custom-call | tf_op jit(solution)/shard_map/gather_schur/pallas_call | solution.py:356
  238.8 2.9 %copy.10 = f32[1,256,6656]{2,1,0:T(8,128)} copy(f32[1,256,6656]{2,1,0:T(8,128)S(1)} %bitcast.26) | data formatting | bytes 13631488
  (5 shorter events, 0.0 us)
Async XLA Ops:
  141.6 2.3 copy-start
  143.9 1.4 copy-start.1
  145.3 1.4 copy-start.2
